TPU v7x, 128 devices: a whole 4x4x4 slice. The times are simulated.
128 devices in a mesh: ctx: 32 (over y, x, core), head: 4 (over z).
Axes of the slice: x: 4, y: 4, z: 4, core: 2. Of those that a mesh axis runs over, the one named last changes fastest.
Arguments:
- q_lin: float32 [8192, 4096], P('ctx', 'head'), may hold values from -6 to 6
- k_lin: float32 [8192, 4096], P('ctx', 'head'), may hold values from -0.9722718 to 0.9722718
- v_lin: float32 [8192, 4096], P('ctx', 'head'), may hold values from -201 to 201
- log_decay: float32 [32, 8192], P('head', 'ctx'), may hold values from -1 to 0
- lin_gain: float32 [4096], P('head'), may hold values from 0.1 to 1.9
- q_soft: float32 [8192, 6144], P('ctx', 'head'), may hold values from -36 to 36
- k_soft: float32 [8192, 1024], P('ctx', 'head'), may hold values from -4 to 4
- v_soft: float32 [8192, 1024], P('ctx', 'head'), may hold values from -6 to 6
Outputs:
- lin_out: float32 [8192, 4096], P('ctx', 'head')
- soft_out: float32 [8192, 6144], P('ctx', 'head')
All inputs are finite; a program needn't handle non-finite values.
Results may differ from a plain program's by a relative error of at most 0.0003.
Values sent between devices are 32-bit elements; how exact they have to be, the bound alone decides.
A program may use at most 128 MiB of HBM per device.

v0:
```python
import math
import jax
import jax.numpy as jnp
from jax import lax
from jax.sharding import PartitionSpec as P

HD = 128
LH = 32
HIGHEST = lax.Precision.HIGHEST
NEGATIVE = -1e30
EPSILON = 1e-05


def entering(value, axis, combine, identity):
    count, mine = (lax.axis_size(axis), lax.axis_index(axis))
    everything = jax.tree.map(lambda part: lax.all_gather(part, axis), value)
    start = jax.tree.map(
        lambda part, zero: jnp.broadcast_to(jnp.asarray(zero, part.dtype), part.shape),
        value,
        identity,
    )

    def turn(k, before):
        reached = k < mine
        new = combine(before, jax.tree.map(lambda part: part[k], everything))
        return jax.tree.map(lambda a, b: jnp.where(reached, a, b), new, before)

    return lax.fori_loop(0, count, turn, start)


def block_terms(queries, key_rows, value_rows, log_rates):
    length = queries.shape[0]
    cumulative = jnp.cumsum(log_rates, axis=1)
    positions = jnp.arange(length)
    causal = (positions[:, None] >= positions[None, :])[None]
    decay_gaps = cumulative[:, :, None] - cumulative[:, None, :]
    weights = jnp.where(causal, jnp.exp(jnp.where(causal, decay_gaps, 0.0)), 0.0)
    scores = jnp.einsum("thd,shd->hts", queries, key_rows, precision=HIGHEST)
    inside = jnp.einsum("hts,shd->thd", scores * weights, value_rows, precision=HIGHEST)
    block_total = cumulative[:, -1]
    trailing = jnp.exp(block_total[:, None] - cumulative)
    scaled_keys = key_rows * jnp.transpose(trailing)[:, :, None]
    local_state = jnp.einsum("shd,she->hde", scaled_keys, value_rows, precision=HIGHEST)
    leading = jnp.transpose(jnp.exp(cumulative))[:, :, None]
    return (inside, leading, block_total, local_state)


def attend(partial_value, query_rows, query_pos, key_slab, value_slab, key_pos, score_scale):
    old_max, old_total, weighted = partial_value
    scores = jnp.einsum("tkgd,skd->kgts", query_rows, key_slab, precision=HIGHEST) * score_scale
    visible = (key_pos[None, :] <= query_pos[:, None])[None, None]
    scores = jnp.where(visible, scores, NEGATIVE)
    new_max = jnp.maximum(old_max, jnp.max(scores, axis=3))
    weights = jnp.where(visible, jnp.exp(scores - new_max[..., None]), 0.0)
    shrink = jnp.exp(old_max - new_max)
    new_total = old_total * shrink + jnp.sum(weights, axis=3)
    weighted = weighted * shrink[..., None] + jnp.einsum(
        "kgts,skd->kgtd", weights, value_slab, precision=HIGHEST
    )
    return (new_max, new_total, weighted)


def soft_layer(query_sets, k_soft, v_soft, score_scale):
    kv_heads = k_soft.shape[1] // HD
    initial = []
    for query_rows, query_pos in query_sets:
        shape = (query_rows.shape[1], query_rows.shape[2], query_rows.shape[0])
        initial.append(
            (
                jnp.full(shape, NEGATIVE, jnp.float32),
                jnp.zeros(shape, jnp.float32),
                jnp.zeros(shape + (HD,), jnp.float32),
            )
        )
    initial = tuple(initial)
    key_rows = lax.all_gather(k_soft, "ctx", axis=0, tiled=True)
    value_rows = lax.all_gather(v_soft, "ctx", axis=0, tiled=True)
    shard_rows = key_rows.shape[0]
    key_block = math.gcd(shard_rows, 512)
    key_rows = key_rows.reshape(shard_rows // key_block, key_block, kv_heads, HD)
    value_rows = value_rows.reshape(shard_rows // key_block, key_block, kv_heads, HD)

    def visit(block_index, partials):
        key_slab = lax.dynamic_index_in_dim(key_rows, block_index, 0, keepdims=False)
        value_slab = lax.dynamic_index_in_dim(value_rows, block_index, 0, keepdims=False)
        first_key = block_index * key_block
        key_pos = first_key + jnp.arange(key_block)
        updated = []
        for (query_rows, query_pos), partial_value in zip(query_sets, partials):

            def engage(current, query_rows=query_rows, query_pos=query_pos):
                return attend(
                    current, query_rows, query_pos, key_slab, value_slab, key_pos, score_scale
                )

            def remain(current):
                return current

            updated.append(lax.cond(first_key <= jnp.max(query_pos), engage, remain, partial_value))
        return tuple(updated)

    finals = lax.fori_loop(0, shard_rows // key_block, visit, initial)
    results = []
    for final in finals:
        maxima, totals, weighted = final
        merged = weighted / totals[..., None]
        row_count = merged.shape[2]
        results.append(jnp.transpose(merged, (2, 0, 1, 3)).reshape(row_count, -1))
    return results


def body(q_lin, k_lin, v_lin, log_decay, lin_gain, q_soft, k_soft, v_soft):
    row_count = q_lin.shape[0]
    head_count = log_decay.shape[0]
    position = lax.axis_index("ctx")
    queries = q_lin.reshape(row_count, head_count, HD)
    key_rows = k_lin.reshape(row_count, head_count, HD)
    value_rows = v_lin.reshape(row_count, head_count, HD)
    inside, leading, block_total, local_state = block_terms(
        queries, key_rows, value_rows, log_decay
    )

    def chain_step(earlier, later):
        return (earlier[0] + later[0], jnp.exp(later[0])[:, None, None] * earlier[1] + later[1])

    identity = (jnp.zeros_like(block_total), jnp.zeros_like(local_state))
    prefix_pair = entering((block_total, local_state), "ctx", chain_step, identity)
    prior_state = prefix_pair[1]
    linear = inside + leading * jnp.einsum("thd,hde->the", queries, prior_state, precision=HIGHEST)
    linear = linear.reshape(row_count, head_count * HD)
    energy = lax.psum(jnp.sum(linear * linear, axis=1, keepdims=True), "head")
    lin_out = linear * lax.rsqrt(energy / (LH * HD) + EPSILON) * lin_gain
    score_scale = 1.0 / math.sqrt(HD)
    kv_heads = k_soft.shape[1] // HD
    group_size = q_soft.shape[1] // (kv_heads * HD)
    soft_queries = q_soft.reshape(row_count, kv_heads, group_size, HD)
    query_pos = position * row_count + jnp.arange(row_count)
    soft_out = soft_layer([(soft_queries, query_pos)], k_soft, v_soft, score_scale)[0]
    return (lin_out, soft_out)


def solution(mesh):
    return jax.shard_map(
        body,
        mesh=mesh,
        in_specs=(
            P("ctx", "head"),
            P("ctx", "head"),
            P("ctx", "head"),
            P("head", "ctx"),
            P("head"),
            P("ctx", "head"),
            P("ctx", "head"),
            P("ctx", "head"),
        ),
        out_specs=(P("ctx", "head"), P("ctx", "head")),
        check_vma=False,
    )
```

profile of v0, /device:TPU:30, one launch (start us, length us, event | category | flops | bytes accessed | tf_op | source)
XLA Modules:
  0.0 573.1 jit_solution(4927016760311225648)
XLA Ops:
  17.5 59.2 %all-reduce = f32[256]{0:T(256)S(1)} all-reduce(f32[256]{0:T(256)S(1)} %dynamic-update-slice), channel_id=2, replica_groups=mesh['ctx'=32,'head'=4] {'ctx'}, use_global_device_ids=true, to_apply=%add | all-reduce | flops 256 | bytes 2048
  86.8 10.8 %reshape.135 = f32[16,512,2,128]{3,2,1,0:T(2,128)} reshape(f32[8192,256]{1,0:T(8,128)} %all-gather.6.cloned.1.call-done) | data formatting | bytes 16777216 | tf_op jit(solution)/shard_map/reshape | solution.py:80
  97.6 8.1 %copy.66 = f32[16,512,2,128]{3,1,2,0:T(8,128)} copy(f32[16,512,2,128]{3,2,1,0:T(2,128)} %reshape.135) | data formatting | bytes 16777216
  105.7 12.2 %all-gather.8.cloned.1.call-done = f32[8192,256]{1,0:T(8,128)} async-done(((f32[256,256]{1,0:T(8,128)}), f32[8192,256]{1,0:T(8,128)}) %all-gather.8.cloned.1.call-update) | async-done | bytes 8388624 | tf_op jit(solution)/shard_map/all_gather | solution.py:77
  117.9 10.8 %reshape.136 = f32[16,512,2,128]{3,2,1,0:T(2,128)} reshape(f32[8192,256]{1,0:T(8,128)} %all-gather.8.cloned.1.call-done) | data formatting | bytes 16777216 | tf_op jit(solution)/shard_map/reshape | solution.py:81
  128.7 7.9 %copy.68 = f32[16,512,2,128]{3,1,2,0:T(8,128)} copy(f32[16,512,2,128]{3,2,1,0:T(2,128)} %reshape.136) | data formatting | bytes 16777216
  137.9 363.9 %while.33 = (s32[]{:T(128)}, f32[2,6,256]{2,1,0:T(8,128)S(1)}, f32[2,6,256]{2,1,0:T(8,128)S(1)}, f32[2,6,256,128]{3,2,1,0:T(8,128)}, s32[]{:T(128)}, /*index=5*/...) while((s32[]{:T(128)}, f32[2,6,256]{2,1,0:T(8,128)S(1)}, ...), condition=%wide.region_12.13_spmd.clone, body=%wide.region_7.0_spmd.clone.sunk | while | flops 4851637248 | bytes 37959000 | solution.py:102
  138.4 22.2 %conditional.3 = ((f32[2,6,256]{2,1,0:T(8,128)S(1)}, f32[2,6,256]{2,1,0:T(8,128)S(1)}, f32[2,6,256,128]{3,2,1,0:T(8,128)})) conditional(s32[]{:T(128)} %convert_element_type.10, (f32[2,6,256]{2,1,0:T(8,128)S(1)}, f32[2,6,256]{2,1,0:T(8,128)S(1)}, f32[2,6,256,128]{3,2,1,0:T(8,128)}) %tuple.98, (s32[]{:T(128)}, s32[512]{0:T(512)S(1)}, s32[]{:T(128)}, ...), branch_computations={%region_8.8_spmd, %region_9.11_spmd} | conditional | flops 4851637248 | bytes 37955680 | solution.py:99
  138.7 7.0 %fusion.2 = (f32[2,6,256]{2,1,0:T(8,128)S(1)}, f32[2,512,256,6]{2,1,3,0:T(8,128)S(1)}) fusion(pred[256,512]{0,1:T(8,128)(4,1)S(1)} %broadcast_compare_fusion, f32[256,2,6,128]{3,0,2,1:T(8,128)S(1)} %get-tuple-element.399, f32[16,512,2,128]{3,1,2,0:T(8,128)} %get-tuple-element.397, s32[]{:T(128)} %get-tuple-element.398), kind=kOutput, calls=%fused_computation.3 | convolution fusion | flops 2420634624 | bytes 8532480 | tf_op jit(solution)/shard_map/while/body/eval_jaxpr/cond/branch_1_fun/tkgd,skd->kgts/dot_general | solution.py:50
  147.2 12.2 %multiply_add_fusion = f32[2,6,256,128]{3,2,1,0:T(8,128)S(1)} fusion(f32[2,6,256,128]{3,2,1,0:T(8,128)S(1)} %copy-done.2, f32[2,512,256,6]{2,1,3,0:T(8,128)S(1)} %get-tuple-element.535, f32[2,6,256]{2,1,0:T(8,128)S(1)} %max.6, pred[256,512]{0,1:T(8,128)(4,1)S(1)} %broadcast_compare_fusion, f32[2,6,256]{2,1,0:T(8,128)S(1)} %get-tuple-element.531, ...), kind=kOutput, calls=%fused_computation.11 | convolution fusion | flops 2422996992 | bytes 10117632 | tf_op jit(solution)/shard_map/while/body/eval_jaxpr/cond/branch_1_fun/kgts,skd->kgtd/dot_general | solution.py:57
  161.2 22.2 %conditional.3 = ((f32[2,6,256]{2,1,0:T(8,128)S(1)}, f32[2,6,256]{2,1,0:T(8,128)S(1)}, f32[2,6,256,128]{3,2,1,0:T(8,128)})) conditional(s32[]{:T(128)} %convert_element_type.10, (f32[2,6,256]{2,1,0:T(8,128)S(1)}, f32[2,6,256]{2,1,0:T(8,128)S(1)}, f32[2,6,256,128]{3,2,1,0:T(8,128)}) %tuple.98, (s32[]{:T(128)}, s32[512]{0:T(512)S(1)}, s32[]{:T(128)}, ...), branch_computations={%region_8.8_spmd, %region_9.11_spmd} | conditional | flops 4851637248 | bytes 37955680 | solution.py:99
  161.4 7.0 %fusion.2 = (f32[2,6,256]{2,1,0:T(8,128)S(1)}, f32[2,512,256,6]{2,1,3,0:T(8,128)S(1)}) fusion(pred[256,512]{0,1:T(8,128)(4,1)S(1)} %broadcast_compare_fusion, f32[256,2,6,128]{3,0,2,1:T(8,128)S(1)} %get-tuple-element.399, f32[16,512,2,128]{3,1,2,0:T(8,128)} %get-tuple-element.397, s32[]{:T(128)} %get-tuple-element.398), kind=kOutput, calls=%fused_computation.3 | convolution fusion | flops 2420634624 | bytes 8532480 | tf_op jit(solution)/shard_map/while/body/eval_jaxpr/cond/branch_1_fun/tkgd,skd->kgts/dot_general | solution.py:50
  170.0 12.2 %multiply_add_fusion = f32[2,6,256,128]{3,2,1,0:T(8,128)S(1)} fusion(f32[2,6,256,128]{3,2,1,0:T(8,128)S(1)} %copy-done.2, f32[2,512,256,6]{2,1,3,0:T(8,128)S(1)} %get-tuple-element.535, f32[2,6,256]{2,1,0:T(8,128)S(1)} %max.6, pred[256,512]{0,1:T(8,128)(4,1)S(1)} %broadcast_compare_fusion, f32[2,6,256]{2,1,0:T(8,128)S(1)} %get-tuple-element.531, ...), kind=kOutput, calls=%fused_computation.11 | convolution fusion | flops 2422996992 | bytes 10117632 | tf_op jit(solution)/shard_map/while/body/eval_jaxpr/cond/branch_1_fun/kgts,skd->kgtd/dot_general | solution.py:57
  183.9 22.2 %conditional.3 = ((f32[2,6,256]{2,1,0:T(8,128)S(1)}, f32[2,6,256]{2,1,0:T(8,128)S(1)}, f32[2,6,256,128]{3,2,1,0:T(8,128)})) conditional(s32[]{:T(128)} %convert_element_type.10, (f32[2,6,256]{2,1,0:T(8,128)S(1)}, f32[2,6,256]{2,1,0:T(8,128)S(1)}, f32[2,6,256,128]{3,2,1,0:T(8,128)}) %tuple.98, (s32[]{:T(128)}, s32[512]{0:T(512)S(1)}, s32[]{:T(128)}, ...), branch_computations={%region_8.8_spmd, %region_9.11_spmd} | conditional | flops 4851637248 | bytes 37955680 | solution.py:99
  184.1 7.0 %fusion.2 = (f32[2,6,256]{2,1,0:T(8,128)S(1)}, f32[2,512,256,6]{2,1,3,0:T(8,128)S(1)}) fusion(pred[256,512]{0,1:T(8,128)(4,1)S(1)} %broadcast_compare_fusion, f32[256,2,6,128]{3,0,2,1:T(8,128)S(1)} %get-tuple-element.399, f32[16,512,2,128]{3,1,2,0:T(8,128)} %get-tuple-element.397, s32[]{:T(128)} %get-tuple-element.398), kind=kOutput, calls=%fused_computation.3 | convolution fusion | flops 2420634624 | bytes 8532480 | tf_op jit(solution)/shard_map/while/body/eval_jaxpr/cond/branch_1_fun/tkgd,skd->kgts/dot_general | solution.py:50
  192.7 12.2 %multiply_add_fusion = f32[2,6,256,128]{3,2,1,0:T(8,128)S(1)} fusion(f32[2,6,256,128]{3,2,1,0:T(8,128)S(1)} %copy-done.2, f32[2,512,256,6]{2,1,3,0:T(8,128)S(1)} %get-tuple-element.535, f32[2,6,256]{2,1,0:T(8,128)S(1)} %max.6, pred[256,512]{0,1:T(8,128)(4,1)S(1)} %broadcast_compare_fusion, f32[2,6,256]{2,1,0:T(8,128)S(1)} %get-tuple-element.531, ...), kind=kOutput, calls=%fused_computation.11 | convolution fusion | flops 2422996992 | bytes 10117632 | tf_op jit(solution)/shard_map/while/body/eval_jaxpr/cond/branch_1_fun/kgts,skd->kgtd/dot_general | solution.py:57
  206.7 22.2 %conditional.3 = ((f32[2,6,256]{2,1,0:T(8,128)S(1)}, f32[2,6,256]{2,1,0:T(8,128)S(1)}, f32[2,6,256,128]{3,2,1,0:T(8,128)})) conditional(s32[]{:T(128)} %convert_element_type.10, (f32[2,6,256]{2,1,0:T(8,128)S(1)}, f32[2,6,256]{2,1,0:T(8,128)S(1)}, f32[2,6,256,128]{3,2,1,0:T(8,128)}) %tuple.98, (s32[]{:T(128)}, s32[512]{0:T(512)S(1)}, s32[]{:T(128)}, ...), branch_computations={%region_8.8_spmd, %region_9.11_spmd} | conditional | flops 4851637248 | bytes 37955680 | solution.py:99
  215.5 12.2 %multiply_add_fusion = f32[2,6,256,128]{3,2,1,0:T(8,128)S(1)} fusion(f32[2,6,256,128]{3,2,1,0:T(8,128)S(1)} %copy-done.2, f32[2,512,256,6]{2,1,3,0:T(8,128)S(1)} %get-tuple-element.535, f32[2,6,256]{2,1,0:T(8,128)S(1)} %max.6, pred[256,512]{0,1:T(8,128)(4,1)S(1)} %broadcast_compare_fusion, f32[2,6,256]{2,1,0:T(8,128)S(1)} %get-tuple-element.531, ...), kind=kOutput, calls=%fused_computation.11 | convolution fusion | flops 2422996992 | bytes 10117632 | tf_op jit(solution)/shard_map/while/body/eval_jaxpr/cond/branch_1_fun/kgts,skd->kgtd/dot_general | solution.py:57
  229.4 22.2 %conditional.3 = ((f32[2,6,256]{2,1,0:T(8,128)S(1)}, f32[2,6,256]{2,1,0:T(8,128)S(1)}, f32[2,6,256,128]{3,2,1,0:T(8,128)})) conditional(s32[]{:T(128)} %convert_element_type.10, (f32[2,6,256]{2,1,0:T(8,128)S(1)}, f32[2,6,256]{2,1,0:T(8,128)S(1)}, f32[2,6,256,128]{3,2,1,0:T(8,128)}) %tuple.98, (s32[]{:T(128)}, s32[512]{0:T(512)S(1)}, s32[]{:T(128)}, ...), branch_computations={%region_8.8_spmd, %region_9.11_spmd} | conditional | flops 4851637248 | bytes 37955680 | solution.py:99
  229.6 7.0 %fusion.2 = (f32[2,6,256]{2,1,0:T(8,128)S(1)}, f32[2,512,256,6]{2,1,3,0:T(8,128)S(1)}) fusion(pred[256,512]{0,1:T(8,128)(4,1)S(1)} %broadcast_compare_fusion, f32[256,2,6,128]{3,0,2,1:T(8,128)S(1)} %get-tuple-element.399, f32[16,512,2,128]{3,1,2,0:T(8,128)} %get-tuple-element.397, s32[]{:T(128)} %get-tuple-element.398), kind=kOutput, calls=%fused_computation.3 | convolution fusion | flops 2420634624 | bytes 8532480 | tf_op jit(solution)/shard_map/while/body/eval_jaxpr/cond/branch_1_fun/tkgd,skd->kgts/dot_general | solution.py:50
  238.2 12.2 %multiply_add_fusion = f32[2,6,256,128]{3,2,1,0:T(8,128)S(1)} fusion(f32[2,6,256,128]{3,2,1,0:T(8,128)S(1)} %copy-done.2, f32[2,512,256,6]{2,1,3,0:T(8,128)S(1)} %get-tuple-element.535, f32[2,6,256]{2,1,0:T(8,128)S(1)} %max.6, pred[256,512]{0,1:T(8,128)(4,1)S(1)} %broadcast_compare_fusion, f32[2,6,256]{2,1,0:T(8,128)S(1)} %get-tuple-element.531, ...), kind=kOutput, calls=%fused_computation.11 | convolution fusion | flops 2422996992 | bytes 10117632 | tf_op jit(solution)/shard_map/while/body/eval_jaxpr/cond/branch_1_fun/kgts,skd->kgtd/dot_general | solution.py:57
  252.2 22.2 %conditional.3 = ((f32[2,6,256]{2,1,0:T(8,128)S(1)}, f32[2,6,256]{2,1,0:T(8,128)S(1)}, f32[2,6,256,128]{3,2,1,0:T(8,128)})) conditional(s32[]{:T(128)} %convert_element_type.10, (f32[2,6,256]{2,1,0:T(8,128)S(1)}, f32[2,6,256]{2,1,0:T(8,128)S(1)}, f32[2,6,256,128]{3,2,1,0:T(8,128)}) %tuple.98, (s32[]{:T(128)}, s32[512]{0:T(512)S(1)}, s32[]{:T(128)}, ...), branch_computations={%region_8.8_spmd, %region_9.11_spmd} | conditional | flops 4851637248 | bytes 37955680 | solution.py:99
  261.0 12.2 %multiply_add_fusion = f32[2,6,256,128]{3,2,1,0:T(8,128)S(1)} fusion(f32[2,6,256,128]{3,2,1,0:T(8,128)S(1)} %copy-done.2, f32[2,512,256,6]{2,1,3,0:T(8,128)S(1)} %get-tuple-element.535, f32[2,6,256]{2,1,0:T(8,128)S(1)} %max.6, pred[256,512]{0,1:T(8,128)(4,1)S(1)} %broadcast_compare_fusion, f32[2,6,256]{2,1,0:T(8,128)S(1)} %get-tuple-element.531, ...), kind=kOutput, calls=%fused_computation.11 | convolution fusion | flops 2422996992 | bytes 10117632 | tf_op jit(solution)/shard_map/while/body/eval_jaxpr/cond/branch_1_fun/kgts,skd->kgtd/dot_general | solution.py:57
  274.9 22.2 %conditional.3 = ((f32[2,6,256]{2,1,0:T(8,128)S(1)}, f32[2,6,256]{2,1,0:T(8,128)S(1)}, f32[2,6,256,128]{3,2,1,0:T(8,128)})) conditional(s32[]{:T(128)} %convert_element_type.10, (f32[2,6,256]{2,1,0:T(8,128)S(1)}, f32[2,6,256]{2,1,0:T(8,128)S(1)}, f32[2,6,256,128]{3,2,1,0:T(8,128)}) %tuple.98, (s32[]{:T(128)}, s32[512]{0:T(512)S(1)}, s32[]{:T(128)}, ...), branch_computations={%region_8.8_spmd, %region_9.11_spmd} | conditional | flops 4851637248 | bytes 37955680 | solution.py:99
  275.1 7.0 %fusion.2 = (f32[2,6,256]{2,1,0:T(8,128)S(1)}, f32[2,512,256,6]{2,1,3,0:T(8,128)S(1)}) fusion(pred[256,512]{0,1:T(8,128)(4,1)S(1)} %broadcast_compare_fusion, f32[256,2,6,128]{3,0,2,1:T(8,128)S(1)} %get-tuple-element.399, f32[16,512,2,128]{3,1,2,0:T(8,128)} %get-tuple-element.397, s32[]{:T(128)} %get-tuple-element.398), kind=kOutput, calls=%fused_computation.3 | convolution fusion | flops 2420634624 | bytes 8532480 | tf_op jit(solution)/shard_map/while/body/eval_jaxpr/cond/branch_1_fun/tkgd,skd->kgts/dot_general | solution.py:50
  283.7 12.2 %multiply_add_fusion = f32[2,6,256,128]{3,2,1,0:T(8,128)S(1)} fusion(f32[2,6,256,128]{3,2,1,0:T(8,128)S(1)} %copy-done.2, f32[2,512,256,6]{2,1,3,0:T(8,128)S(1)} %get-tuple-element.535, f32[2,6,256]{2,1,0:T(8,128)S(1)} %max.6, pred[256,512]{0,1:T(8,128)(4,1)S(1)} %broadcast_compare_fusion, f32[2,6,256]{2,1,0:T(8,128)S(1)} %get-tuple-element.531, ...), kind=kOutput, calls=%fused_computation.11 | convolution fusion | flops 2422996992 | bytes 10117632 | tf_op jit(solution)/shard_map/while/body/eval_jaxpr/cond/branch_1_fun/kgts,skd->kgtd/dot_general | solution.py:57
  297.6 22.2 %conditional.3 = ((f32[2,6,256]{2,1,0:T(8,128)S(1)}, f32[2,6,256]{2,1,0:T(8,128)S(1)}, f32[2,6,256,128]{3,2,1,0:T(8,128)})) conditional(s32[]{:T(128)} %convert_element_type.10, (f32[2,6,256]{2,1,0:T(8,128)S(1)}, f32[2,6,256]{2,1,0:T(8,128)S(1)}, f32[2,6,256,128]{3,2,1,0:T(8,128)}) %tuple.98, (s32[]{:T(128)}, s32[512]{0:T(512)S(1)}, s32[]{:T(128)}, ...), branch_computations={%region_8.8_spmd, %region_9.11_spmd} | conditional | flops 4851637248 | bytes 37955680 | solution.py:99
  306.4 12.2 %multiply_add_fusion = f32[2,6,256,128]{3,2,1,0:T(8,128)S(1)} fusion(f32[2,6,256,128]{3,2,1,0:T(8,128)S(1)} %copy-done.2, f32[2,512,256,6]{2,1,3,0:T(8,128)S(1)} %get-tuple-element.535, f32[2,6,256]{2,1,0:T(8,128)S(1)} %max.6, pred[256,512]{0,1:T(8,128)(4,1)S(1)} %broadcast_compare_fusion, f32[2,6,256]{2,1,0:T(8,128)S(1)} %get-tuple-element.531, ...), kind=kOutput, calls=%fused_computation.11 | convolution fusion | flops 2422996992 | bytes 10117632 | tf_op jit(solution)/shard_map/while/body/eval_jaxpr/cond/branch_1_fun/kgts,skd->kgtd/dot_general | solution.py:57
  320.4 22.2 %conditional.3 = ((f32[2,6,256]{2,1,0:T(8,128)S(1)}, f32[2,6,256]{2,1,0:T(8,128)S(1)}, f32[2,6,256,128]{3,2,1,0:T(8,128)})) conditional(s32[]{:T(128)} %convert_element_type.10, (f32[2,6,256]{2,1,0:T(8,128)S(1)}, f32[2,6,256]{2,1,0:T(8,128)S(1)}, f32[2,6,256,128]{3,2,1,0:T(8,128)}) %tuple.98, (s32[]{:T(128)}, s32[512]{0:T(512)S(1)}, s32[]{:T(128)}, ...), branch_computations={%region_8.8_spmd, %region_9.11_spmd} | conditional | flops 4851637248 | bytes 37955680 | solution.py:99
  320.6 7.0 %fusion.2 = (f32[2,6,256]{2,1,0:T(8,128)S(1)}, f32[2,512,256,6]{2,1,3,0:T(8,128)S(1)}) fusion(pred[256,512]{0,1:T(8,128)(4,1)S(1)} %broadcast_compare_fusion, f32[256,2,6,128]{3,0,2,1:T(8,128)S(1)} %get-tuple-element.399, f32[16,512,2,128]{3,1,2,0:T(8,128)} %get-tuple-element.397, s32[]{:T(128)} %get-tuple-element.398), kind=kOutput, calls=%fused_computation.3 | convolution fusion | flops 2420634624 | bytes 8532480 | tf_op jit(solution)/shard_map/while/body/eval_jaxpr/cond/branch_1_fun/tkgd,skd->kgts/dot_general | solution.py:50
  329.2 12.2 %multiply_add_fusion = f32[2,6,256,128]{3,2,1,0:T(8,128)S(1)} fusion(f32[2,6,256,128]{3,2,1,0:T(8,128)S(1)} %copy-done.2, f32[2,512,256,6]{2,1,3,0:T(8,128)S(1)} %get-tuple-element.535, f32[2,6,256]{2,1,0:T(8,128)S(1)} %max.6, pred[256,512]{0,1:T(8,128)(4,1)S(1)} %broadcast_compare_fusion, f32[2,6,256]{2,1,0:T(8,128)S(1)} %get-tuple-element.531, ...), kind=kOutput, calls=%fused_computation.11 | convolution fusion | flops 2422996992 | bytes 10117632 | tf_op jit(solution)/shard_map/while/body/eval_jaxpr/cond/branch_1_fun/kgts,skd->kgtd/dot_general | solution.py:57
  343.1 22.2 %conditional.3 = ((f32[2,6,256]{2,1,0:T(8,128)S(1)}, f32[2,6,256]{2,1,0:T(8,128)S(1)}, f32[2,6,256,128]{3,2,1,0:T(8,128)})) conditional(s32[]{:T(128)} %convert_element_type.10, (f32[2,6,256]{2,1,0:T(8,128)S(1)}, f32[2,6,256]{2,1,0:T(8,128)S(1)}, f32[2,6,256,128]{3,2,1,0:T(8,128)}) %tuple.98, (s32[]{:T(128)}, s32[512]{0:T(512)S(1)}, s32[]{:T(128)}, ...), branch_computations={%region_8.8_spmd, %region_9.11_spmd} | conditional | flops 4851637248 | bytes 37955680 | solution.py:99
  351.9 12.2 %multiply_add_fusion = f32[2,6,256,128]{3,2,1,0:T(8,128)S(1)} fusion(f32[2,6,256,128]{3,2,1,0:T(8,128)S(1)} %copy-done.2, f32[2,512,256,6]{2,1,3,0:T(8,128)S(1)} %get-tuple-element.535, f32[2,6,256]{2,1,0:T(8,128)S(1)} %max.6, pred[256,512]{0,1:T(8,128)(4,1)S(1)} %broadcast_compare_fusion, f32[2,6,256]{2,1,0:T(8,128)S(1)} %get-tuple-element.531, ...), kind=kOutput, calls=%fused_computation.11 | convolution fusion | flops 2422996992 | bytes 10117632 | tf_op jit(solution)/shard_map/while/body/eval_jaxpr/cond/branch_1_fun/kgts,skd->kgtd/dot_general | solution.py:57
  365.9 22.2 %conditional.3 = ((f32[2,6,256]{2,1,0:T(8,128)S(1)}, f32[2,6,256]{2,1,0:T(8,128)S(1)}, f32[2,6,256,128]{3,2,1,0:T(8,128)})) conditional(s32[]{:T(128)} %convert_element_type.10, (f32[2,6,256]{2,1,0:T(8,128)S(1)}, f32[2,6,256]{2,1,0:T(8,128)S(1)}, f32[2,6,256,128]{3,2,1,0:T(8,128)}) %tuple.98, (s32[]{:T(128)}, s32[512]{0:T(512)S(1)}, s32[]{:T(128)}, ...), branch_computations={%region_8.8_spmd, %region_9.11_spmd} | conditional | flops 4851637248 | bytes 37955680 | solution.py:99
  366.1 7.0 %fusion.2 = (f32[2,6,256]{2,1,0:T(8,128)S(1)}, f32[2,512,256,6]{2,1,3,0:T(8,128)S(1)}) fusion(pred[256,512]{0,1:T(8,128)(4,1)S(1)} %broadcast_compare_fusion, f32[256,2,6,128]{3,0,2,1:T(8,128)S(1)} %get-tuple-element.399, f32[16,512,2,128]{3,1,2,0:T(8,128)} %get-tuple-element.397, s32[]{:T(128)} %get-tuple-element.398), kind=kOutput, calls=%fused_computation.3 | convolution fusion | flops 2420634624 | bytes 8532480 | tf_op jit(solution)/shard_map/while/body/eval_jaxpr/cond/branch_1_fun/tkgd,skd->kgts/dot_general | solution.py:50
  374.7 12.2 %multiply_add_fusion = f32[2,6,256,128]{3,2,1,0:T(8,128)S(1)} fusion(f32[2,6,256,128]{3,2,1,0:T(8,128)S(1)} %copy-done.2, f32[2,512,256,6]{2,1,3,0:T(8,128)S(1)} %get-tuple-element.535, f32[2,6,256]{2,1,0:T(8,128)S(1)} %max.6, pred[256,512]{0,1:T(8,128)(4,1)S(1)} %broadcast_compare_fusion, f32[2,6,256]{2,1,0:T(8,128)S(1)} %get-tuple-element.531, ...), kind=kOutput, calls=%fused_computation.11 | convolution fusion | flops 2422996992 | bytes 10117632 | tf_op jit(solution)/shard_map/while/body/eval_jaxpr/cond/branch_1_fun/kgts,skd->kgtd/dot_general | solution.py:57
  388.6 22.2 %conditional.3 = ((f32[2,6,256]{2,1,0:T(8,128)S(1)}, f32[2,6,256]{2,1,0:T(8,128)S(1)}, f32[2,6,256,128]{3,2,1,0:T(8,128)})) conditional(s32[]{:T(128)} %convert_element_type.10, (f32[2,6,256]{2,1,0:T(8,128)S(1)}, f32[2,6,256]{2,1,0:T(8,128)S(1)}, f32[2,6,256,128]{3,2,1,0:T(8,128)}) %tuple.98, (s32[]{:T(128)}, s32[512]{0:T(512)S(1)}, s32[]{:T(128)}, ...), branch_computations={%region_8.8_spmd, %region_9.11_spmd} | conditional | flops 4851637248 | bytes 37955680 | solution.py:99
  397.4 12.2 %multiply_add_fusion = f32[2,6,256,128]{3,2,1,0:T(8,128)S(1)} fusion(f32[2,6,256,128]{3,2,1,0:T(8,128)S(1)} %copy-done.2, f32[2,512,256,6]{2,1,3,0:T(8,128)S(1)} %get-tuple-element.535, f32[2,6,256]{2,1,0:T(8,128)S(1)} %max.6, pred[256,512]{0,1:T(8,128)(4,1)S(1)} %broadcast_compare_fusion, f32[2,6,256]{2,1,0:T(8,128)S(1)} %get-tuple-element.531, ...), kind=kOutput, calls=%fused_computation.11 | convolution fusion | flops 2422996992 | bytes 10117632 | tf_op jit(solution)/shard_map/while/body/eval_jaxpr/cond/branch_1_fun/kgts,skd->kgtd/dot_general | solution.py:57
  411.3 22.2 %conditional.3 = ((f32[2,6,256]{2,1,0:T(8,128)S(1)}, f32[2,6,256]{2,1,0:T(8,128)S(1)}, f32[2,6,256,128]{3,2,1,0:T(8,128)})) conditional(s32[]{:T(128)} %convert_element_type.10, (f32[2,6,256]{2,1,0:T(8,128)S(1)}, f32[2,6,256]{2,1,0:T(8,128)S(1)}, f32[2,6,256,128]{3,2,1,0:T(8,128)}) %tuple.98, (s32[]{:T(128)}, s32[512]{0:T(512)S(1)}, s32[]{:T(128)}, ...), branch_computations={%region_8.8_spmd, %region_9.11_spmd} | conditional | flops 4851637248 | bytes 37955680 | solution.py:99
  420.1 12.2 %multiply_add_fusion = f32[2,6,256,128]{3,2,1,0:T(8,128)S(1)} fusion(f32[2,6,256,128]{3,2,1,0:T(8,128)S(1)} %copy-done.2, f32[2,512,256,6]{2,1,3,0:T(8,128)S(1)} %get-tuple-element.535, f32[2,6,256]{2,1,0:T(8,128)S(1)} %max.6, pred[256,512]{0,1:T(8,128)(4,1)S(1)} %broadcast_compare_fusion, f32[2,6,256]{2,1,0:T(8,128)S(1)} %get-tuple-element.531, ...), kind=kOutput, calls=%fused_computation.11 | convolution fusion | flops 2422996992 | bytes 10117632 | tf_op jit(solution)/shard_map/while/body/eval_jaxpr/cond/branch_1_fun/kgts,skd->kgtd/dot_general | solution.py:57
  434.1 22.2 %conditional.3 = ((f32[2,6,256]{2,1,0:T(8,128)S(1)}, f32[2,6,256]{2,1,0:T(8,128)S(1)}, f32[2,6,256,128]{3,2,1,0:T(8,128)})) conditional(s32[]{:T(128)} %convert_element_type.10, (f32[2,6,256]{2,1,0:T(8,128)S(1)}, f32[2,6,256]{2,1,0:T(8,128)S(1)}, f32[2,6,256,128]{3,2,1,0:T(8,128)}) %tuple.98, (s32[]{:T(128)}, s32[512]{0:T(512)S(1)}, s32[]{:T(128)}, ...), branch_computations={%region_8.8_spmd, %region_9.11_spmd} | conditional | flops 4851637248 | bytes 37955680 | solution.py:99
  442.9 12.2 %multiply_add_fusion = f32[2,6,256,128]{3,2,1,0:T(8,128)S(1)} fusion(f32[2,6,256,128]{3,2,1,0:T(8,128)S(1)} %copy-done.2, f32[2,512,256,6]{2,1,3,0:T(8,128)S(1)} %get-tuple-element.535, f32[2,6,256]{2,1,0:T(8,128)S(1)} %max.6, pred[256,512]{0,1:T(8,128)(4,1)S(1)} %broadcast_compare_fusion, f32[2,6,256]{2,1,0:T(8,128)S(1)} %get-tuple-element.531, ...), kind=kOutput, calls=%fused_computation.11 | convolution fusion | flops 2422996992 | bytes 10117632 | tf_op jit(solution)/shard_map/while/body/eval_jaxpr/cond/branch_1_fun/kgts,skd->kgtd/dot_general | solution.py:57
  456.8 22.2 %conditional.3 = ((f32[2,6,256]{2,1,0:T(8,128)S(1)}, f32[2,6,256]{2,1,0:T(8,128)S(1)}, f32[2,6,256,128]{3,2,1,0:T(8,128)})) conditional(s32[]{:T(128)} %convert_element_type.10, (f32[2,6,256]{2,1,0:T(8,128)S(1)}, f32[2,6,256]{2,1,0:T(8,128)S(1)}, f32[2,6,256,128]{3,2,1,0:T(8,128)}) %tuple.98, (s32[]{:T(128)}, s32[512]{0:T(512)S(1)}, s32[]{:T(128)}, ...), branch_computations={%region_8.8_spmd, %region_9.11_spmd} | conditional | flops 4851637248 | bytes 37955680 | solution.py:99
  465.6 12.2 %multiply_add_fusion = f32[2,6,256,128]{3,2,1,0:T(8,128)S(1)} fusion(f32[2,6,256,128]{3,2,1,0:T(8,128)S(1)} %copy-done.2, f32[2,512,256,6]{2,1,3,0:T(8,128)S(1)} %get-tuple-element.535, f32[2,6,256]{2,1,0:T(8,128)S(1)} %max.6, pred[256,512]{0,1:T(8,128)(4,1)S(1)} %broadcast_compare_fusion, f32[2,6,256]{2,1,0:T(8,128)S(1)} %get-tuple-element.531, ...), kind=kOutput, calls=%fused_computation.11 | convolution fusion | flops 2422996992 | bytes 10117632 | tf_op jit(solution)/shard_map/while/body/eval_jaxpr/cond/branch_1_fun/kgts,skd->kgtd/dot_general | solution.py:57
  479.6 22.2 %conditional.3 = ((f32[2,6,256]{2,1,0:T(8,128)S(1)}, f32[2,6,256]{2,1,0:T(8,128)S(1)}, f32[2,6,256,128]{3,2,1,0:T(8,128)})) conditional(s32[]{:T(128)} %convert_element_type.10, (f32[2,6,256]{2,1,0:T(8,128)S(1)}, f32[2,6,256]{2,1,0:T(8,128)S(1)}, f32[2,6,256,128]{3,2,1,0:T(8,128)}) %tuple.98, (s32[]{:T(128)}, s32[512]{0:T(512)S(1)}, s32[]{:T(128)}, ...), branch_computations={%region_8.8_spmd, %region_9.11_spmd} | conditional | flops 4851637248 | bytes 37955680 | solution.py:99
  488.4 12.2 %multiply_add_fusion = f32[2,6,256,128]{3,2,1,0:T(8,128)S(1)} fusion(f32[2,6,256,128]{3,2,1,0:T(8,128)S(1)} %copy-done.2, f32[2,512,256,6]{2,1,3,0:T(8,128)S(1)} %get-tuple-element.535, f32[2,6,256]{2,1,0:T(8,128)S(1)} %max.6, pred[256,512]{0,1:T(8,128)(4,1)S(1)} %broadcast_compare_fusion, f32[2,6,256]{2,1,0:T(8,128)S(1)} %get-tuple-element.531, ...), kind=kOutput, calls=%fused_computation.11 | convolution fusion | flops 2422996992 | bytes 10117632 | tf_op jit(solution)/shard_map/while/body/eval_jaxpr/cond/branch_1_fun/kgts,skd->kgtd/dot_general | solution.py:57
  508.1 38.9 %while.34 = (s32[]{:T(128)}, f32[8,128,128]{2,1,0:T(8,128)S(1)}, s32[]{:T(128)}, f32[32,8]{1,0:T(8,128)S(1)}, f32[32,8,128,128]{3,2,1,0:T(8,128)}, /*index=5*/s32[]{:T(128)}, s32[]{:T(128)}) while((s32[]{:T(128)}, f32[8,128,128]{2,1,0:T(8,128)S(1)}, s32[]{:T(128)}, f32[32,8]{1,0:T(8,128)S(1)}, f32[32,8,128,128]{3,2,1,0:T(8,128)}, ...), condition=%wide.region_3.4_spmd.clone, body=%wide.region_2.3_spmd.clone.sunk | while | flops 524292 | bytes 1573065 | solution.py:28
  554.7 10.7 %psum.7 = f32[256,1]{0,1:T(1,128)S(1)} all-reduce(f32[256,1]{0,1:T(1,128)S(1)} %bitcast.97), channel_id=1, replica_groups=mesh['ctx'=32,'head'=4] {'head'}, use_global_device_ids=true, to_apply=%region_5.6 | all-reduce | flops 256 | bytes 2048 | tf_op jit(solution)/shard_map/psum | solution.py:131
  (327 shorter events, 182.5 us)
Async XLA Ops:
  7.2 75.3 %copy-start = (f32[256,1024]{1,0:T(8,128)S(1)}, f32[256,1024]{1,0:T(8,128)}, u32[]{:S(2)}) copy-start(f32[256,1024]{1,0:T(8,128)} %param.14) | copy-start | bytes 3145732
  7.2 79.7 %all-gather.6.cloned.1.call-start = ((), (), s32[]{:S(2)}) async-start(), calls=%async_computation | async-start | bytes 8650752 | tf_op jit(solution)/shard_map/all_gather | solution.py:76
  7.9 110.0 %all-gather.8.cloned.1.call-start = ((), (), s32[]{:S(2)}) async-start(), calls=%async_computation.1 | async-start | bytes 8650752 | tf_op jit(solution)/shard_map/all_gather | solution.py:77
  8.7 499.4 %all-gather.10.cloned.1.call-start = ((), (), s32[]{:S(2)}) async-start(), calls=%async_computation.2 | async-start | bytes 17301504 | tf_op jit(solution)/shard_map/all_gather | solution.py:16
  11.7 3.6 copy-start.1
  138.6 8.6 %copy-start.2 = (f32[2,6,256,128]{3,2,1,0:T(8,128)S(1)}, f32[2,6,256,128]{3,2,1,0:T(8,128)}, u32[]{:S(2)}) copy-start(f32[2,6,256,128]{3,2,1,0:T(8,128)} %get-tuple-element.401) | copy-start | bytes 4718596 | tf_op jit(solution)/shard_map/while/body/eval_jaxpr/cond
  159.5 1.1 copy-start.3
  161.4 8.6 %copy-start.2 = (f32[2,6,256,128]{3,2,1,0:T(8,128)S(1)}, f32[2,6,256,128]{3,2,1,0:T(8,128)}, u32[]{:S(2)}) copy-start(f32[2,6,256,128]{3,2,1,0:T(8,128)} %get-tuple-element.401) | copy-start | bytes 4718596 | tf_op jit(solution)/shard_map/while/body/eval_jaxpr/cond
  182.2 1.1 copy-start.3
  184.1 8.6 %copy-start.2 = (f32[2,6,256,128]{3,2,1,0:T(8,128)S(1)}, f32[2,6,256,128]{3,2,1,0:T(8,128)}, u32[]{:S(2)}) copy-start(f32[2,6,256,128]{3,2,1,0:T(8,128)} %get-tuple-element.401) | copy-start | bytes 4718596 | tf_op jit(solution)/shard_map/while/body/eval_jaxpr/cond
  205.0 1.1 copy-start.3
  206.9 8.6 %copy-start.2 = (f32[2,6,256,128]{3,2,1,0:T(8,128)S(1)}, f32[2,6,256,128]{3,2,1,0:T(8,128)}, u32[]{:S(2)}) copy-start(f32[2,6,256,128]{3,2,1,0:T(8,128)} %get-tuple-element.401) | copy-start | bytes 4718596 | tf_op jit(solution)/shard_map/while/body/eval_jaxpr/cond
  227.7 1.1 copy-start.3
  229.6 8.6 %copy-start.2 = (f32[2,6,256,128]{3,2,1,0:T(8,128)S(1)}, f32[2,6,256,128]{3,2,1,0:T(8,128)}, u32[]{:S(2)}) copy-start(f32[2,6,256,128]{3,2,1,0:T(8,128)} %get-tuple-element.401) | copy-start | bytes 4718596 | tf_op jit(solution)/shard_map/while/body/eval_jaxpr/cond
  250.4 1.1 copy-start.3
  252.4 8.6 %copy-start.2 = (f32[2,6,256,128]{3,2,1,0:T(8,128)S(1)}, f32[2,6,256,128]{3,2,1,0:T(8,128)}, u32[]{:S(2)}) copy-start(f32[2,6,256,128]{3,2,1,0:T(8,128)} %get-tuple-element.401) | copy-start | bytes 4718596 | tf_op jit(solution)/shard_map/while/body/eval_jaxpr/cond
  273.2 1.1 copy-start.3
  275.1 8.6 %copy-start.2 = (f32[2,6,256,128]{3,2,1,0:T(8,128)S(1)}, f32[2,6,256,128]{3,2,1,0:T(8,128)}, u32[]{:S(2)}) copy-start(f32[2,6,256,128]{3,2,1,0:T(8,128)} %get-tuple-element.401) | copy-start | bytes 4718596 | tf_op jit(solution)/shard_map/while/body/eval_jaxpr/cond
  295.9 1.1 copy-start.3
  297.8 8.6 %copy-start.2 = (f32[2,6,256,128]{3,2,1,0:T(8,128)S(1)}, f32[2,6,256,128]{3,2,1,0:T(8,128)}, u32[]{:S(2)}) copy-start(f32[2,6,256,128]{3,2,1,0:T(8,128)} %get-tuple-element.401) | copy-start | bytes 4718596 | tf_op jit(solution)/shard_map/while/body/eval_jaxpr/cond
  318.7 1.1 copy-start.3
  320.6 8.6 %copy-start.2 = (f32[2,6,256,128]{3,2,1,0:T(8,128)S(1)}, f32[2,6,256,128]{3,2,1,0:T(8,128)}, u32[]{:S(2)}) copy-start(f32[2,6,256,128]{3,2,1,0:T(8,128)} %get-tuple-element.401) | copy-start | bytes 4718596 | tf_op jit(solution)/shard_map/while/body/eval_jaxpr/cond
  341.4 1.1 copy-start.3
  343.3 8.6 %copy-start.2 = (f32[2,6,256,128]{3,2,1,0:T(8,128)S(1)}, f32[2,6,256,128]{3,2,1,0:T(8,128)}, u32[]{:S(2)}) copy-start(f32[2,6,256,128]{3,2,1,0:T(8,128)} %get-tuple-element.401) | copy-start | bytes 4718596 | tf_op jit(solution)/shard_map/while/body/eval_jaxpr/cond
  364.1 1.1 copy-start.3
  366.1 8.6 %copy-start.2 = (f32[2,6,256,128]{3,2,1,0:T(8,128)S(1)}, f32[2,6,256,128]{3,2,1,0:T(8,128)}, u32[]{:S(2)}) copy-start(f32[2,6,256,128]{3,2,1,0:T(8,128)} %get-tuple-element.401) | copy-start | bytes 4718596 | tf_op jit(solution)/shard_map/while/body/eval_jaxpr/cond
  386.9 1.1 copy-start.3
  388.8 8.6 %copy-start.2 = (f32[2,6,256,128]{3,2,1,0:T(8,128)S(1)}, f32[2,6,256,128]{3,2,1,0:T(8,128)}, u32[]{:S(2)}) copy-start(f32[2,6,256,128]{3,2,1,0:T(8,128)} %get-tuple-element.401) | copy-start | bytes 4718596 | tf_op jit(solution)/shard_map/while/body/eval_jaxpr/cond
  409.6 1.1 copy-start.3
  411.5 8.6 %copy-start.2 = (f32[2,6,256,128]{3,2,1,0:T(8,128)S(1)}, f32[2,6,256,128]{3,2,1,0:T(8,128)}, u32[]{:S(2)}) copy-start(f32[2,6,256,128]{3,2,1,0:T(8,128)} %get-tuple-element.401) | copy-start | bytes 4718596 | tf_op jit(solution)/shard_map/while/body/eval_jaxpr/cond
  432.4 1.1 copy-start.3
  434.3 8.6 %copy-start.2 = (f32[2,6,256,128]{3,2,1,0:T(8,128)S(1)}, f32[2,6,256,128]{3,2,1,0:T(8,128)}, u32[]{:S(2)}) copy-start(f32[2,6,256,128]{3,2,1,0:T(8,128)} %get-tuple-element.401) | copy-start | bytes 4718596 | tf_op jit(solution)/shard_map/while/body/eval_jaxpr/cond
  455.1 1.1 copy-start.3
  457.0 8.6 %copy-start.2 = (f32[2,6,256,128]{3,2,1,0:T(8,128)S(1)}, f32[2,6,256,128]{3,2,1,0:T(8,128)}, u32[]{:S(2)}) copy-start(f32[2,6,256,128]{3,2,1,0:T(8,128)} %get-tuple-element.401) | copy-start | bytes 4718596 | tf_op jit(solution)/shard_map/while/body/eval_jaxpr/cond
  477.9 1.1 copy-start.3
  479.8 8.6 %copy-start.2 = (f32[2,6,256,128]{3,2,1,0:T(8,128)S(1)}, f32[2,6,256,128]{3,2,1,0:T(8,128)}, u32[]{:S(2)}) copy-start(f32[2,6,256,128]{3,2,1,0:T(8,128)} %get-tuple-element.401) | copy-start | bytes 4718596 | tf_op jit(solution)/shard_map/while/body/eval_jaxpr/cond
  500.6 1.1 copy-start.3
  505.0 43.1 %copy-start.4 = (f32[256,1024]{1,0:T(8,128)S(1)}, f32[256,1024]{1,0:T(8,128)}, u32[]{:S(2)}) copy-start(f32[256,1024]{1,0:T(8,128)} %param.16) | copy-start | bytes 3145732
  546.9 18.5 %copy-start.5 = (f32[1024]{0:T(1024)S(1)}, f32[1024]{0:T(1024)}, u32[]{:S(2)}) copy-start(f32[1024]{0:T(1024)} %param.18) | copy-start | bytes 12292
Sparse Core Ops, SparseCore 0:
  10.3 52.9 all-gather.5
  65.5 52.3 all-gather.7
  120.2 71.9 all-gather.9
where the time goes:
time: 577 us; the launch traced here: 573 us
  matrix products  322 us (56%)
  local copies, waits for them, and re-layouts  72.5 us (13%)
  blocking collectives  69.9 us (12%)
  other arithmetic  68.9 us (12%)
  between operations  14.5 us (3%)
  waiting for transfers between devices  13.6 us (2%)
  loops' own time  11.8 us (2%)
    dot_general x16, matrix products, attend(): jnp.einsum('kgts,skd->kgtd', weights, value_slab, precision=HIGHEST)  195 us
    dot_general x16, matrix products, attend(): jnp.einsum('tkgd,skd->kgts', query_rows, key_slab, precision=HIGHEST)  113 us
    unnamed x1, blocking collectives  59.2 us
    select_n x32, other arithmetic, turn(): return jax.tree.map(lambda a, b: jnp.where(reached, a, b), new, before)  37.5 us
    unnamed x16, local copies, waits for them, and re-layouts  25.6 us
    reduce_sum x16, other arithmetic, attend(): new_total = old_total * shrink + jnp.sum(weights, axis=3)  24 us
    cond x80, local copies, waits for them, and re-layouts  18.2 us
    all_gather x1, waiting for transfers between devices, soft_layer(): value_rows = lax.all_gather(v_soft, 'ctx', axis=0, tiled=True)  12.2 us
  transfers between devices with their start and end apart: 3, of which 1 were waited for; matrix products, arithmetic and copies ran while one was open for 69% of the time, Pallas kernels for 0%

commit v1 on v0

--- a/solution.py
+++ b/solution.py
@@ -73,8 +73,11 @@
             )
         )
     initial = tuple(initial)
-    key_rows = lax.all_gather(k_soft, "ctx", axis=0, tiled=True)
-    value_rows = lax.all_gather(v_soft, "ctx", axis=0, tiled=True)
+    key_rows, value_rows = jnp.split(
+        lax.all_gather(jnp.concatenate([k_soft, v_soft], axis=1), "ctx", axis=0, tiled=True),
+        [k_soft.shape[1]],
+        axis=1,
+    )
     shard_rows = key_rows.shape[0]
     key_block = math.gcd(shard_rows, 512)
     key_rows = key_rows.reshape(shard_rows // key_block, key_block, kv_heads, HD)

time: 577 us -> 594 us (1.029)
  local copies, waits for them, and re-layouts: 72.5 us -> 82.3 us
    split x0 -> x1, local copies, waits for them, and re-layouts: none -> 11.5 us  [soft_layer(): jnp.split(lax.all_gather(jnp.concatenate([k_soft, v_soft], axis=1), 'ctx'...]
    all_gather x2 -> x1, waiting for transfers between devices: 12.2 us -> 15.1 us  [soft_layer(): lax.all_gather(jnp.concatenate([k_soft, v_soft], axis=1), 'ctx', axis=0,...]
    unnamed x16 -> x18, local copies, waits for them, and re-layouts: 25.6 us -> 24.1 us
  transfers between devices with their start and end apart: 3 -> 2, of which waited for: 1 -> 1; matrix products, arithmetic and copies ran while one was open for 69% -> 10% of each run, Pallas kernels for 0% -> 0%
where the time goes in v1:
time: 594 us; the launch traced here: 590 us
  matrix products  322 us (54%)
  local copies, waits for them, and re-layouts  82.3 us (14%)
  other arithmetic  72.4 us (12%)
  blocking collectives  72.1 us (12%)
  waiting for transfers between devices  15.1 us (3%)
  between operations  14.8 us (2%)
  loops' own time  11.9 us (2%)
    dot_general x16, matrix products, attend(): jnp.einsum('kgts,skd->kgtd', weights, value_slab, precision=HIGHEST)  195 us
    dot_general x16, matrix products, attend(): jnp.einsum('tkgd,skd->kgts', query_rows, key_slab, precision=HIGHEST)  113 us
    unnamed x1, blocking collectives  60 us
    select_n x32, other arithmetic, turn(): return jax.tree.map(lambda a, b: jnp.where(reached, a, b), new, before)  37.8 us
    reduce_sum x16, other arithmetic, attend(): new_total = old_total * shrink + jnp.sum(weights, axis=3)  24.1 us
    unnamed x18, local copies, waits for them, and re-layouts  24.1 us
    cond x80, local copies, waits for them, and re-layouts  18.2 us
    all_gather x1, waiting for transfers between devices, soft_layer(): lax.all_gather(jnp.concatenate([k_soft, v_soft], axis=1), 'ctx', axis=0,...  15.1 us
  transfers between devices with their start and end apart: 2, of which 1 were waited for; matrix products, arithmetic and copies ran while one was open for 10% of the time, Pallas kernels for 0%

profile of v1, /device:TPU:30, one launch (start us, length us, event | category | flops | bytes accessed | tf_op | source)
XLA Modules:
  0.0 590.4 jit_solution(15811000384148834762)
XLA Ops:
  17.8 60.0 %all-reduce = f32[256]{0:T(256)S(1)} all-reduce(f32[256]{0:T(256)S(1)} %dynamic-update-slice), channel_id=2, replica_groups=mesh['ctx'=32,'head'=4] {'ctx'}, use_global_device_ids=true, to_apply=%add | all-reduce | flops 256 | bytes 2048
  87.8 39.1 %while.34 = (s32[]{:T(128)}, f32[8,128,128]{2,1,0:T(8,128)S(1)}, s32[]{:T(128)}, f32[32,8]{1,0:T(8,128)S(1)}, f32[32,8,128,128]{3,2,1,0:T(8,128)}, /*index=5*/s32[]{:T(128)}, s32[]{:T(128)}) while((s32[]{:T(128)}, f32[8,128,128]{2,1,0:T(8,128)S(1)}, s32[]{:T(128)}, f32[32,8]{1,0:T(8,128)S(1)}, f32[32,8,128,128]{3,2,1,0:T(8,128)}, ...), condition=%wide.region_3.4_spmd.clone, body=%wide.region_2.3_spmd.clone.sunk | while | flops 524292 | bytes 1573065 | solution.py:28
  134.0 12.1 %psum.7 = f32[256,1]{0,1:T(1,128)S(1)} all-reduce(f32[256,1]{0,1:T(1,128)S(1)} %bitcast.98), channel_id=1, replica_groups=mesh['ctx'=32,'head'=4] {'head'}, use_global_device_ids=true, to_apply=%region_5.6 | all-reduce | flops 256 | bytes 2048 | tf_op jit(solution)/shard_map/psum | solution.py:134
  146.1 15.1 %all-gather.5.cloned.1.call-done = f32[8192,512]{1,0:T(8,128)} async-done(((f32[256,512]{1,0:T(8,128)}), f32[8192,512]{1,0:T(8,128)}) %all-gather.5.cloned.1.call-update) | async-done | bytes 16777232 | tf_op jit(solution)/shard_map/all_gather | solution.py:77
  161.2 11.5 %fusion.51 = (f32[8192,256]{1,0:T(8,128)}, f32[8192,256]{1,0:T(8,128)}) fusion(f32[8192,512]{1,0:T(8,128)} %all-gather.5.cloned.1.call-done), kind=kLoop, calls=%fused_computation.69 | loop fusion | bytes 33554432 | tf_op jit(solution)/shard_map/split | solution.py:76
  172.7 10.8 %reshape.135 = f32[16,512,2,128]{3,2,1,0:T(2,128)} reshape(f32[8192,256]{1,0:T(8,128)} %get-tuple-element.537) | data formatting | bytes 16777216 | tf_op jit(solution)/shard_map/reshape | solution.py:83
  183.5 7.7 %copy.66 = f32[16,512,2,128]{3,1,2,0:T(8,128)} copy(f32[16,512,2,128]{3,2,1,0:T(2,128)} %reshape.135) | data formatting | bytes 16777216
  191.2 10.8 %reshape.136 = f32[16,512,2,128]{3,2,1,0:T(2,128)} reshape(f32[8192,256]{1,0:T(8,128)} %get-tuple-element.536) | data formatting | bytes 16777216 | tf_op jit(solution)/shard_map/reshape | solution.py:84
  201.9 7.6 %copy.68 = f32[16,512,2,128]{3,1,2,0:T(8,128)} copy(f32[16,512,2,128]{3,2,1,0:T(2,128)} %reshape.136) | data formatting | bytes 16777216
  210.9 364.0 %while.33 = (s32[]{:T(128)}, f32[2,6,256]{2,1,0:T(8,128)S(1)}, f32[2,6,256]{2,1,0:T(8,128)S(1)}, f32[2,6,256,128]{3,2,1,0:T(8,128)}, s32[]{:T(128)}, /*index=5*/...) while((s32[]{:T(128)}, f32[2,6,256]{2,1,0:T(8,128)S(1)}, ...), condition=%wide.region_12.13_spmd.clone, body=%wide.region_7.0_spmd.clone.sunk | while | flops 4851637248 | bytes 37959000 | solution.py:105
  211.5 22.2 %conditional.3 = ((f32[2,6,256]{2,1,0:T(8,128)S(1)}, f32[2,6,256]{2,1,0:T(8,128)S(1)}, f32[2,6,256,128]{3,2,1,0:T(8,128)})) conditional(s32[]{:T(128)} %convert_element_type.10, (f32[2,6,256]{2,1,0:T(8,128)S(1)}, f32[2,6,256]{2,1,0:T(8,128)S(1)}, f32[2,6,256,128]{3,2,1,0:T(8,128)}) %tuple.99, (s32[]{:T(128)}, s32[512]{0:T(512)S(1)}, s32[]{:T(128)}, ...), branch_computations={%region_8.8_spmd, %region_9.11_spmd} | conditional | flops 4851637248 | bytes 37955680 | solution.py:102
  211.7 7.0 %fusion.2 = (f32[2,6,256]{2,1,0:T(8,128)S(1)}, f32[2,512,256,6]{2,1,3,0:T(8,128)S(1)}) fusion(pred[256,512]{0,1:T(8,128)(4,1)S(1)} %broadcast_compare_fusion, f32[256,2,6,128]{3,0,2,1:T(8,128)S(1)} %get-tuple-element.399, f32[16,512,2,128]{3,1,2,0:T(8,128)} %get-tuple-element.397, s32[]{:T(128)} %get-tuple-element.398), kind=kOutput, calls=%fused_computation.3 | convolution fusion | flops 2420634624 | bytes 8532480 | tf_op jit(solution)/shard_map/while/body/eval_jaxpr/cond/branch_1_fun/tkgd,skd->kgts/dot_general | solution.py:50
  220.3 12.2 %multiply_add_fusion = f32[2,6,256,128]{3,2,1,0:T(8,128)S(1)} fusion(f32[2,6,256,128]{3,2,1,0:T(8,128)S(1)} %copy-done.3, f32[2,512,256,6]{2,1,3,0:T(8,128)S(1)} %get-tuple-element.535, f32[2,6,256]{2,1,0:T(8,128)S(1)} %max.6, pred[256,512]{0,1:T(8,128)(4,1)S(1)} %broadcast_compare_fusion, f32[2,6,256]{2,1,0:T(8,128)S(1)} %get-tuple-element.531, ...), kind=kOutput, calls=%fused_computation.11 | convolution fusion | flops 2422996992 | bytes 10117632 | tf_op jit(solution)/shard_map/while/body/eval_jaxpr/cond/branch_1_fun/kgts,skd->kgtd/dot_general | solution.py:57
  234.2 22.2 %conditional.3 = ((f32[2,6,256]{2,1,0:T(8,128)S(1)}, f32[2,6,256]{2,1,0:T(8,128)S(1)}, f32[2,6,256,128]{3,2,1,0:T(8,128)})) conditional(s32[]{:T(128)} %convert_element_type.10, (f32[2,6,256]{2,1,0:T(8,128)S(1)}, f32[2,6,256]{2,1,0:T(8,128)S(1)}, f32[2,6,256,128]{3,2,1,0:T(8,128)}) %tuple.99, (s32[]{:T(128)}, s32[512]{0:T(512)S(1)}, s32[]{:T(128)}, ...), branch_computations={%region_8.8_spmd, %region_9.11_spmd} | conditional | flops 4851637248 | bytes 37955680 | solution.py:102
  243.0 12.2 %multiply_add_fusion = f32[2,6,256,128]{3,2,1,0:T(8,128)S(1)} fusion(f32[2,6,256,128]{3,2,1,0:T(8,128)S(1)} %copy-done.3, f32[2,512,256,6]{2,1,3,0:T(8,128)S(1)} %get-tuple-element.535, f32[2,6,256]{2,1,0:T(8,128)S(1)} %max.6, pred[256,512]{0,1:T(8,128)(4,1)S(1)} %broadcast_compare_fusion, f32[2,6,256]{2,1,0:T(8,128)S(1)} %get-tuple-element.531, ...), kind=kOutput, calls=%fused_computation.11 | convolution fusion | flops 2422996992 | bytes 10117632 | tf_op jit(solution)/shard_map/while/body/eval_jaxpr/cond/branch_1_fun/kgts,skd->kgtd/dot_general | solution.py:57
  257.0 22.2 %conditional.3 = ((f32[2,6,256]{2,1,0:T(8,128)S(1)}, f32[2,6,256]{2,1,0:T(8,128)S(1)}, f32[2,6,256,128]{3,2,1,0:T(8,128)})) conditional(s32[]{:T(128)} %convert_element_type.10, (f32[2,6,256]{2,1,0:T(8,128)S(1)}, f32[2,6,256]{2,1,0:T(8,128)S(1)}, f32[2,6,256,128]{3,2,1,0:T(8,128)}) %tuple.99, (s32[]{:T(128)}, s32[512]{0:T(512)S(1)}, s32[]{:T(128)}, ...), branch_computations={%region_8.8_spmd, %region_9.11_spmd} | conditional | flops 4851637248 | bytes 37955680 | solution.py:102
  257.2 7.0 %fusion.2 = (f32[2,6,256]{2,1,0:T(8,128)S(1)}, f32[2,512,256,6]{2,1,3,0:T(8,128)S(1)}) fusion(pred[256,512]{0,1:T(8,128)(4,1)S(1)} %broadcast_compare_fusion, f32[256,2,6,128]{3,0,2,1:T(8,128)S(1)} %get-tuple-element.399, f32[16,512,2,128]{3,1,2,0:T(8,128)} %get-tuple-element.397, s32[]{:T(128)} %get-tuple-element.398), kind=kOutput, calls=%fused_computation.3 | convolution fusion | flops 2420634624 | bytes 8532480 | tf_op jit(solution)/shard_map/while/body/eval_jaxpr/cond/branch_1_fun/tkgd,skd->kgts/dot_general | solution.py:50
  265.8 12.2 %multiply_add_fusion = f32[2,6,256,128]{3,2,1,0:T(8,128)S(1)} fusion(f32[2,6,256,128]{3,2,1,0:T(8,128)S(1)} %copy-done.3, f32[2,512,256,6]{2,1,3,0:T(8,128)S(1)} %get-tuple-element.535, f32[2,6,256]{2,1,0:T(8,128)S(1)} %max.6, pred[256,512]{0,1:T(8,128)(4,1)S(1)} %broadcast_compare_fusion, f32[2,6,256]{2,1,0:T(8,128)S(1)} %get-tuple-element.531, ...), kind=kOutput, calls=%fused_computation.11 | convolution fusion | flops 2422996992 | bytes 10117632 | tf_op jit(solution)/shard_map/while/body/eval_jaxpr/cond/branch_1_fun/kgts,skd->kgtd/dot_general | solution.py:57
  279.7 22.2 %conditional.3 = ((f32[2,6,256]{2,1,0:T(8,128)S(1)}, f32[2,6,256]{2,1,0:T(8,128)S(1)}, f32[2,6,256,128]{3,2,1,0:T(8,128)})) conditional(s32[]{:T(128)} %convert_element_type.10, (f32[2,6,256]{2,1,0:T(8,128)S(1)}, f32[2,6,256]{2,1,0:T(8,128)S(1)}, f32[2,6,256,128]{3,2,1,0:T(8,128)}) %tuple.99, (s32[]{:T(128)}, s32[512]{0:T(512)S(1)}, s32[]{:T(128)}, ...), branch_computations={%region_8.8_spmd, %region_9.11_spmd} | conditional | flops 4851637248 | bytes 37955680 | solution.py:102
  288.5 12.2 %multiply_add_fusion = f32[2,6,256,128]{3,2,1,0:T(8,128)S(1)} fusion(f32[2,6,256,128]{3,2,1,0:T(8,128)S(1)} %copy-done.3, f32[2,512,256,6]{2,1,3,0:T(8,128)S(1)} %get-tuple-element.535, f32[2,6,256]{2,1,0:T(8,128)S(1)} %max.6, pred[256,512]{0,1:T(8,128)(4,1)S(1)} %broadcast_compare_fusion, f32[2,6,256]{2,1,0:T(8,128)S(1)} %get-tuple-element.531, ...), kind=kOutput, calls=%fused_computation.11 | convolution fusion | flops 2422996992 | bytes 10117632 | tf_op jit(solution)/shard_map/while/body/eval_jaxpr/cond/branch_1_fun/kgts,skd->kgtd/dot_general | solution.py:57
  302.5 22.2 %conditional.3 = ((f32[2,6,256]{2,1,0:T(8,128)S(1)}, f32[2,6,256]{2,1,0:T(8,128)S(1)}, f32[2,6,256,128]{3,2,1,0:T(8,128)})) conditional(s32[]{:T(128)} %convert_element_type.10, (f32[2,6,256]{2,1,0:T(8,128)S(1)}, f32[2,6,256]{2,1,0:T(8,128)S(1)}, f32[2,6,256,128]{3,2,1,0:T(8,128)}) %tuple.99, (s32[]{:T(128)}, s32[512]{0:T(512)S(1)}, s32[]{:T(128)}, ...), branch_computations={%region_8.8_spmd, %region_9.11_spmd} | conditional | flops 4851637248 | bytes 37955680 | solution.py:102
  302.7 7.0 %fusion.2 = (f32[2,6,256]{2,1,0:T(8,128)S(1)}, f32[2,512,256,6]{2,1,3,0:T(8,128)S(1)}) fusion(pred[256,512]{0,1:T(8,128)(4,1)S(1)} %broadcast_compare_fusion, f32[256,2,6,128]{3,0,2,1:T(8,128)S(1)} %get-tuple-element.399, f32[16,512,2,128]{3,1,2,0:T(8,128)} %get-tuple-element.397, s32[]{:T(128)} %get-tuple-element.398), kind=kOutput, calls=%fused_computation.3 | convolution fusion | flops 2420634624 | bytes 8532480 | tf_op jit(solution)/shard_map/while/body/eval_jaxpr/cond/branch_1_fun/tkgd,skd->kgts/dot_general | solution.py:50
  311.3 12.2 %multiply_add_fusion = f32[2,6,256,128]{3,2,1,0:T(8,128)S(1)} fusion(f32[2,6,256,128]{3,2,1,0:T(8,128)S(1)} %copy-done.3, f32[2,512,256,6]{2,1,3,0:T(8,128)S(1)} %get-tuple-element.535, f32[2,6,256]{2,1,0:T(8,128)S(1)} %max.6, pred[256,512]{0,1:T(8,128)(4,1)S(1)} %broadcast_compare_fusion, f32[2,6,256]{2,1,0:T(8,128)S(1)} %get-tuple-element.531, ...), kind=kOutput, calls=%fused_computation.11 | convolution fusion | flops 2422996992 | bytes 10117632 | tf_op jit(solution)/shard_map/while/body/eval_jaxpr/cond/branch_1_fun/kgts,skd->kgtd/dot_general | solution.py:57
  325.2 22.2 %conditional.3 = ((f32[2,6,256]{2,1,0:T(8,128)S(1)}, f32[2,6,256]{2,1,0:T(8,128)S(1)}, f32[2,6,256,128]{3,2,1,0:T(8,128)})) conditional(s32[]{:T(128)} %convert_element_type.10, (f32[2,6,256]{2,1,0:T(8,128)S(1)}, f32[2,6,256]{2,1,0:T(8,128)S(1)}, f32[2,6,256,128]{3,2,1,0:T(8,128)}) %tuple.99, (s32[]{:T(128)}, s32[512]{0:T(512)S(1)}, s32[]{:T(128)}, ...), branch_computations={%region_8.8_spmd, %region_9.11_spmd} | conditional | flops 4851637248 | bytes 37955680 | solution.py:102
  334.0 12.2 %multiply_add_fusion = f32[2,6,256,128]{3,2,1,0:T(8,128)S(1)} fusion(f32[2,6,256,128]{3,2,1,0:T(8,128)S(1)} %copy-done.3, f32[2,512,256,6]{2,1,3,0:T(8,128)S(1)} %get-tuple-element.535, f32[2,6,256]{2,1,0:T(8,128)S(1)} %max.6, pred[256,512]{0,1:T(8,128)(4,1)S(1)} %broadcast_compare_fusion, f32[2,6,256]{2,1,0:T(8,128)S(1)} %get-tuple-element.531, ...), kind=kOutput, calls=%fused_computation.11 | convolution fusion | flops 2422996992 | bytes 10117632 | tf_op jit(solution)/shard_map/while/body/eval_jaxpr/cond/branch_1_fun/kgts,skd->kgtd/dot_general | solution.py:57
  348.0 22.2 %conditional.3 = ((f32[2,6,256]{2,1,0:T(8,128)S(1)}, f32[2,6,256]{2,1,0:T(8,128)S(1)}, f32[2,6,256,128]{3,2,1,0:T(8,128)})) conditional(s32[]{:T(128)} %convert_element_type.10, (f32[2,6,256]{2,1,0:T(8,128)S(1)}, f32[2,6,256]{2,1,0:T(8,128)S(1)}, f32[2,6,256,128]{3,2,1,0:T(8,128)}) %tuple.99, (s32[]{:T(128)}, s32[512]{0:T(512)S(1)}, s32[]{:T(128)}, ...), branch_computations={%region_8.8_spmd, %region_9.11_spmd} | conditional | flops 4851637248 | bytes 37955680 | solution.py:102
  348.2 7.0 %fusion.2 = (f32[2,6,256]{2,1,0:T(8,128)S(1)}, f32[2,512,256,6]{2,1,3,0:T(8,128)S(1)}) fusion(pred[256,512]{0,1:T(8,128)(4,1)S(1)} %broadcast_compare_fusion, f32[256,2,6,128]{3,0,2,1:T(8,128)S(1)} %get-tuple-element.399, f32[16,512,2,128]{3,1,2,0:T(8,128)} %get-tuple-element.397, s32[]{:T(128)} %get-tuple-element.398), kind=kOutput, calls=%fused_computation.3 | convolution fusion | flops 2420634624 | bytes 8532480 | tf_op jit(solution)/shard_map/while/body/eval_jaxpr/cond/branch_1_fun/tkgd,skd->kgts/dot_general | solution.py:50
  356.8 12.2 %multiply_add_fusion = f32[2,6,256,128]{3,2,1,0:T(8,128)S(1)} fusion(f32[2,6,256,128]{3,2,1,0:T(8,128)S(1)} %copy-done.3, f32[2,512,256,6]{2,1,3,0:T(8,128)S(1)} %get-tuple-element.535, f32[2,6,256]{2,1,0:T(8,128)S(1)} %max.6, pred[256,512]{0,1:T(8,128)(4,1)S(1)} %broadcast_compare_fusion, f32[2,6,256]{2,1,0:T(8,128)S(1)} %get-tuple-element.531, ...), kind=kOutput, calls=%fused_computation.11 | convolution fusion | flops 2422996992 | bytes 10117632 | tf_op jit(solution)/shard_map/while/body/eval_jaxpr/cond/branch_1_fun/kgts,skd->kgtd/dot_general | solution.py:57
  370.7 22.2 %conditional.3 = ((f32[2,6,256]{2,1,0:T(8,128)S(1)}, f32[2,6,256]{2,1,0:T(8,128)S(1)}, f32[2,6,256,128]{3,2,1,0:T(8,128)})) conditional(s32[]{:T(128)} %convert_element_type.10, (f32[2,6,256]{2,1,0:T(8,128)S(1)}, f32[2,6,256]{2,1,0:T(8,128)S(1)}, f32[2,6,256,128]{3,2,1,0:T(8,128)}) %tuple.99, (s32[]{:T(128)}, s32[512]{0:T(512)S(1)}, s32[]{:T(128)}, ...), branch_computations={%region_8.8_spmd, %region_9.11_spmd} | conditional | flops 4851637248 | bytes 37955680 | solution.py:102
  379.5 12.2 %multiply_add_fusion = f32[2,6,256,128]{3,2,1,0:T(8,128)S(1)} fusion(f32[2,6,256,128]{3,2,1,0:T(8,128)S(1)} %copy-done.3, f32[2,512,256,6]{2,1,3,0:T(8,128)S(1)} %get-tuple-element.535, f32[2,6,256]{2,1,0:T(8,128)S(1)} %max.6, pred[256,512]{0,1:T(8,128)(4,1)S(1)} %broadcast_compare_fusion, f32[2,6,256]{2,1,0:T(8,128)S(1)} %get-tuple-element.531, ...), kind=kOutput, calls=%fused_computation.11 | convolution fusion | flops 2422996992 | bytes 10117632 | tf_op jit(solution)/shard_map/while/body/eval_jaxpr/cond/branch_1_fun/kgts,skd->kgtd/dot_general | solution.py:57
  393.5 22.2 %conditional.3 = ((f32[2,6,256]{2,1,0:T(8,128)S(1)}, f32[2,6,256]{2,1,0:T(8,128)S(1)}, f32[2,6,256,128]{3,2,1,0:T(8,128)})) conditional(s32[]{:T(128)} %convert_element_type.10, (f32[2,6,256]{2,1,0:T(8,128)S(1)}, f32[2,6,256]{2,1,0:T(8,128)S(1)}, f32[2,6,256,128]{3,2,1,0:T(8,128)}) %tuple.99, (s32[]{:T(128)}, s32[512]{0:T(512)S(1)}, s32[]{:T(128)}, ...), branch_computations={%region_8.8_spmd, %region_9.11_spmd} | conditional | flops 4851637248 | bytes 37955680 | solution.py:102
  393.7 7.0 %fusion.2 = (f32[2,6,256]{2,1,0:T(8,128)S(1)}, f32[2,512,256,6]{2,1,3,0:T(8,128)S(1)}) fusion(pred[256,512]{0,1:T(8,128)(4,1)S(1)} %broadcast_compare_fusion, f32[256,2,6,128]{3,0,2,1:T(8,128)S(1)} %get-tuple-element.399, f32[16,512,2,128]{3,1,2,0:T(8,128)} %get-tuple-element.397, s32[]{:T(128)} %get-tuple-element.398), kind=kOutput, calls=%fused_computation.3 | convolution fusion | flops 2420634624 | bytes 8532480 | tf_op jit(solution)/shard_map/while/body/eval_jaxpr/cond/branch_1_fun/tkgd,skd->kgts/dot_general | solution.py:50
  402.3 12.2 %multiply_add_fusion = f32[2,6,256,128]{3,2,1,0:T(8,128)S(1)} fusion(f32[2,6,256,128]{3,2,1,0:T(8,128)S(1)} %copy-done.3, f32[2,512,256,6]{2,1,3,0:T(8,128)S(1)} %get-tuple-element.535, f32[2,6,256]{2,1,0:T(8,128)S(1)} %max.6, pred[256,512]{0,1:T(8,128)(4,1)S(1)} %broadcast_compare_fusion, f32[2,6,256]{2,1,0:T(8,128)S(1)} %get-tuple-element.531, ...), kind=kOutput, calls=%fused_computation.11 | convolution fusion | flops 2422996992 | bytes 10117632 | tf_op jit(solution)/shard_map/while/body/eval_jaxpr/cond/branch_1_fun/kgts,skd->kgtd/dot_general | solution.py:57
  416.2 22.2 %conditional.3 = ((f32[2,6,256]{2,1,0:T(8,128)S(1)}, f32[2,6,256]{2,1,0:T(8,128)S(1)}, f32[2,6,256,128]{3,2,1,0:T(8,128)})) conditional(s32[]{:T(128)} %convert_element_type.10, (f32[2,6,256]{2,1,0:T(8,128)S(1)}, f32[2,6,256]{2,1,0:T(8,128)S(1)}, f32[2,6,256,128]{3,2,1,0:T(8,128)}) %tuple.99, (s32[]{:T(128)}, s32[512]{0:T(512)S(1)}, s32[]{:T(128)}, ...), branch_computations={%region_8.8_spmd, %region_9.11_spmd} | conditional | flops 4851637248 | bytes 37955680 | solution.py:102
  425.0 12.2 %multiply_add_fusion = f32[2,6,256,128]{3,2,1,0:T(8,128)S(1)} fusion(f32[2,6,256,128]{3,2,1,0:T(8,128)S(1)} %copy-done.3, f32[2,512,256,6]{2,1,3,0:T(8,128)S(1)} %get-tuple-element.535, f32[2,6,256]{2,1,0:T(8,128)S(1)} %max.6, pred[256,512]{0,1:T(8,128)(4,1)S(1)} %broadcast_compare_fusion, f32[2,6,256]{2,1,0:T(8,128)S(1)} %get-tuple-element.531, ...), kind=kOutput, calls=%fused_computation.11 | convolution fusion | flops 2422996992 | bytes 10117632 | tf_op jit(solution)/shard_map/while/body/eval_jaxpr/cond/branch_1_fun/kgts,skd->kgtd/dot_general | solution.py:57
  439.0 22.2 %conditional.3 = ((f32[2,6,256]{2,1,0:T(8,128)S(1)}, f32[2,6,256]{2,1,0:T(8,128)S(1)}, f32[2,6,256,128]{3,2,1,0:T(8,128)})) conditional(s32[]{:T(128)} %convert_element_type.10, (f32[2,6,256]{2,1,0:T(8,128)S(1)}, f32[2,6,256]{2,1,0:T(8,128)S(1)}, f32[2,6,256,128]{3,2,1,0:T(8,128)}) %tuple.99, (s32[]{:T(128)}, s32[512]{0:T(512)S(1)}, s32[]{:T(128)}, ...), branch_computations={%region_8.8_spmd, %region_9.11_spmd} | conditional | flops 4851637248 | bytes 37955680 | solution.py:102
  439.2 7.0 %fusion.2 = (f32[2,6,256]{2,1,0:T(8,128)S(1)}, f32[2,512,256,6]{2,1,3,0:T(8,128)S(1)}) fusion(pred[256,512]{0,1:T(8,128)(4,1)S(1)} %broadcast_compare_fusion, f32[256,2,6,128]{3,0,2,1:T(8,128)S(1)} %get-tuple-element.399, f32[16,512,2,128]{3,1,2,0:T(8,128)} %get-tuple-element.397, s32[]{:T(128)} %get-tuple-element.398), kind=kOutput, calls=%fused_computation.3 | convolution fusion | flops 2420634624 | bytes 8532480 | tf_op jit(solution)/shard_map/while/body/eval_jaxpr/cond/branch_1_fun/tkgd,skd->kgts/dot_general | solution.py:50
  447.8 12.2 %multiply_add_fusion = f32[2,6,256,128]{3,2,1,0:T(8,128)S(1)} fusion(f32[2,6,256,128]{3,2,1,0:T(8,128)S(1)} %copy-done.3, f32[2,512,256,6]{2,1,3,0:T(8,128)S(1)} %get-tuple-element.535, f32[2,6,256]{2,1,0:T(8,128)S(1)} %max.6, pred[256,512]{0,1:T(8,128)(4,1)S(1)} %broadcast_compare_fusion, f32[2,6,256]{2,1,0:T(8,128)S(1)} %get-tuple-element.531, ...), kind=kOutput, calls=%fused_computation.11 | convolution fusion | flops 2422996992 | bytes 10117632 | tf_op jit(solution)/shard_map/while/body/eval_jaxpr/cond/branch_1_fun/kgts,skd->kgtd/dot_general | solution.py:57
  461.7 22.2 %conditional.3 = ((f32[2,6,256]{2,1,0:T(8,128)S(1)}, f32[2,6,256]{2,1,0:T(8,128)S(1)}, f32[2,6,256,128]{3,2,1,0:T(8,128)})) conditional(s32[]{:T(128)} %convert_element_type.10, (f32[2,6,256]{2,1,0:T(8,128)S(1)}, f32[2,6,256]{2,1,0:T(8,128)S(1)}, f32[2,6,256,128]{3,2,1,0:T(8,128)}) %tuple.99, (s32[]{:T(128)}, s32[512]{0:T(512)S(1)}, s32[]{:T(128)}, ...), branch_computations={%region_8.8_spmd, %region_9.11_spmd} | conditional | flops 4851637248 | bytes 37955680 | solution.py:102
  470.5 12.2 %multiply_add_fusion = f32[2,6,256,128]{3,2,1,0:T(8,128)S(1)} fusion(f32[2,6,256,128]{3,2,1,0:T(8,128)S(1)} %copy-done.3, f32[2,512,256,6]{2,1,3,0:T(8,128)S(1)} %get-tuple-element.535, f32[2,6,256]{2,1,0:T(8,128)S(1)} %max.6, pred[256,512]{0,1:T(8,128)(4,1)S(1)} %broadcast_compare_fusion, f32[2,6,256]{2,1,0:T(8,128)S(1)} %get-tuple-element.531, ...), kind=kOutput, calls=%fused_computation.11 | convolution fusion | flops 2422996992 | bytes 10117632 | tf_op jit(solution)/shard_map/while/body/eval_jaxpr/cond/branch_1_fun/kgts,skd->kgtd/dot_general | solution.py:57
  484.5 22.2 %conditional.3 = ((f32[2,6,256]{2,1,0:T(8,128)S(1)}, f32[2,6,256]{2,1,0:T(8,128)S(1)}, f32[2,6,256,128]{3,2,1,0:T(8,128)})) conditional(s32[]{:T(128)} %convert_element_type.10, (f32[2,6,256]{2,1,0:T(8,128)S(1)}, f32[2,6,256]{2,1,0:T(8,128)S(1)}, f32[2,6,256,128]{3,2,1,0:T(8,128)}) %tuple.99, (s32[]{:T(128)}, s32[512]{0:T(512)S(1)}, s32[]{:T(128)}, ...), branch_computations={%region_8.8_spmd, %region_9.11_spmd} | conditional | flops 4851637248 | bytes 37955680 | solution.py:102
  493.3 12.2 %multiply_add_fusion = f32[2,6,256,128]{3,2,1,0:T(8,128)S(1)} fusion(f32[2,6,256,128]{3,2,1,0:T(8,128)S(1)} %copy-done.3, f32[2,512,256,6]{2,1,3,0:T(8,128)S(1)} %get-tuple-element.535, f32[2,6,256]{2,1,0:T(8,128)S(1)} %max.6, pred[256,512]{0,1:T(8,128)(4,1)S(1)} %broadcast_compare_fusion, f32[2,6,256]{2,1,0:T(8,128)S(1)} %get-tuple-element.531, ...), kind=kOutput, calls=%fused_computation.11 | convolution fusion | flops 2422996992 | bytes 10117632 | tf_op jit(solution)/shard_map/while/body/eval_jaxpr/cond/branch_1_fun/kgts,skd->kgtd/dot_general | solution.py:57
  507.2 22.2 %conditional.3 = ((f32[2,6,256]{2,1,0:T(8,128)S(1)}, f32[2,6,256]{2,1,0:T(8,128)S(1)}, f32[2,6,256,128]{3,2,1,0:T(8,128)})) conditional(s32[]{:T(128)} %convert_element_type.10, (f32[2,6,256]{2,1,0:T(8,128)S(1)}, f32[2,6,256]{2,1,0:T(8,128)S(1)}, f32[2,6,256,128]{3,2,1,0:T(8,128)}) %tuple.99, (s32[]{:T(128)}, s32[512]{0:T(512)S(1)}, s32[]{:T(128)}, ...), branch_computations={%region_8.8_spmd, %region_9.11_spmd} | conditional | flops 4851637248 | bytes 37955680 | solution.py:102
  516.0 12.2 %multiply_add_fusion = f32[2,6,256,128]{3,2,1,0:T(8,128)S(1)} fusion(f32[2,6,256,128]{3,2,1,0:T(8,128)S(1)} %copy-done.3, f32[2,512,256,6]{2,1,3,0:T(8,128)S(1)} %get-tuple-element.535, f32[2,6,256]{2,1,0:T(8,128)S(1)} %max.6, pred[256,512]{0,1:T(8,128)(4,1)S(1)} %broadcast_compare_fusion, f32[2,6,256]{2,1,0:T(8,128)S(1)} %get-tuple-element.531, ...), kind=kOutput, calls=%fused_computation.11 | convolution fusion | flops 2422996992 | bytes 10117632 | tf_op jit(solution)/shard_map/while/body/eval_jaxpr/cond/branch_1_fun/kgts,skd->kgtd/dot_general | solution.py:57
  530.0 22.2 %conditional.3 = ((f32[2,6,256]{2,1,0:T(8,128)S(1)}, f32[2,6,256]{2,1,0:T(8,128)S(1)}, f32[2,6,256,128]{3,2,1,0:T(8,128)})) conditional(s32[]{:T(128)} %convert_element_type.10, (f32[2,6,256]{2,1,0:T(8,128)S(1)}, f32[2,6,256]{2,1,0:T(8,128)S(1)}, f32[2,6,256,128]{3,2,1,0:T(8,128)}) %tuple.99, (s32[]{:T(128)}, s32[512]{0:T(512)S(1)}, s32[]{:T(128)}, ...), branch_computations={%region_8.8_spmd, %region_9.11_spmd} | conditional | flops 4851637248 | bytes 37955680 | solution.py:102
  538.8 12.2 %multiply_add_fusion = f32[2,6,256,128]{3,2,1,0:T(8,128)S(1)} fusion(f32[2,6,256,128]{3,2,1,0:T(8,128)S(1)} %copy-done.3, f32[2,512,256,6]{2,1,3,0:T(8,128)S(1)} %get-tuple-element.535, f32[2,6,256]{2,1,0:T(8,128)S(1)} %max.6, pred[256,512]{0,1:T(8,128)(4,1)S(1)} %broadcast_compare_fusion, f32[2,6,256]{2,1,0:T(8,128)S(1)} %get-tuple-element.531, ...), kind=kOutput, calls=%fused_computation.11 | convolution fusion | flops 2422996992 | bytes 10117632 | tf_op jit(solution)/shard_map/while/body/eval_jaxpr/cond/branch_1_fun/kgts,skd->kgtd/dot_general | solution.py:57
  552.7 22.2 %conditional.3 = ((f32[2,6,256]{2,1,0:T(8,128)S(1)}, f32[2,6,256]{2,1,0:T(8,128)S(1)}, f32[2,6,256,128]{3,2,1,0:T(8,128)})) conditional(s32[]{:T(128)} %convert_element_type.10, (f32[2,6,256]{2,1,0:T(8,128)S(1)}, f32[2,6,256]{2,1,0:T(8,128)S(1)}, f32[2,6,256,128]{3,2,1,0:T(8,128)}) %tuple.99, (s32[]{:T(128)}, s32[512]{0:T(512)S(1)}, s32[]{:T(128)}, ...), branch_computations={%region_8.8_spmd, %region_9.11_spmd} | conditional | flops 4851637248 | bytes 37955680 | solution.py:102
  561.5 12.2 %multiply_add_fusion = f32[2,6,256,128]{3,2,1,0:T(8,128)S(1)} fusion(f32[2,6,256,128]{3,2,1,0:T(8,128)S(1)} %copy-done.3, f32[2,512,256,6]{2,1,3,0:T(8,128)S(1)} %get-tuple-element.535, f32[2,6,256]{2,1,0:T(8,128)S(1)} %max.6, pred[256,512]{0,1:T(8,128)(4,1)S(1)} %broadcast_compare_fusion, f32[2,6,256]{2,1,0:T(8,128)S(1)} %get-tuple-element.531, ...), kind=kOutput, calls=%fused_computation.11 | convolution fusion | flops 2422996992 | bytes 10117632 | tf_op jit(solution)/shard_map/while/body/eval_jaxpr/cond/branch_1_fun/kgts,skd->kgtd/dot_general | solution.py:57
  (328 shorter events, 190.4 us)
Async XLA Ops:
  7.2 76.3 %copy-start = (f32[256,1024]{1,0:T(8,128)S(1)}, f32[256,1024]{1,0:T(8,128)}, u32[]{:S(2)}) copy-start(f32[256,1024]{1,0:T(8,128)} %param.14) | copy-start | bytes 3145732
  7.2 9.1 %copy-start.6 = (u32[128]{0:T(128)S(1)}, u32[128]{0:T(128)}, u32[]{:S(2)}) copy-start(u32[128]{0:T(128)} %constant.131) | copy-start | bytes 1540
  7.2 80.6 %all-gather.7.cloned.1.call-start = ((), (), s32[]{:S(2)}) async-start(), calls=%async_computation.1 | async-start | bytes 17301504 | tf_op jit(solution)/shard_map/all_gather | solution.py:16
  10.7 70.9 %copy-start.2 = (f32[256,1024]{0,1:T(8,128)}, f32[256,1024]{0,1:T(8,128)S(1)}, u32[]{:S(2)}) copy-start(f32[256,1024]{0,1:T(8,128)S(1)} %copy.79) | copy-start | bytes 3145732
  14.3 146.9 %all-gather.5.cloned.1.call-start = ((), (), s32[]{:S(2)}) async-start(), calls=%async_computation | async-start | bytes 17301504 | tf_op jit(solution)/shard_map/all_gather | solution.py:77
  211.7 8.6 %copy-start.3 = (f32[2,6,256,128]{3,2,1,0:T(8,128)S(1)}, f32[2,6,256,128]{3,2,1,0:T(8,128)}, u32[]{:S(2)}) copy-start(f32[2,6,256,128]{3,2,1,0:T(8,128)} %get-tuple-element.401) | copy-start | bytes 4718596 | tf_op jit(solution)/shard_map/while/body/eval_jaxpr/cond
  232.5 1.1 copy-start.4
  234.4 8.6 %copy-start.3 = (f32[2,6,256,128]{3,2,1,0:T(8,128)S(1)}, f32[2,6,256,128]{3,2,1,0:T(8,128)}, u32[]{:S(2)}) copy-start(f32[2,6,256,128]{3,2,1,0:T(8,128)} %get-tuple-element.401) | copy-start | bytes 4718596 | tf_op jit(solution)/shard_map/while/body/eval_jaxpr/cond
  255.2 1.1 copy-start.4
  257.2 8.6 %copy-start.3 = (f32[2,6,256,128]{3,2,1,0:T(8,128)S(1)}, f32[2,6,256,128]{3,2,1,0:T(8,128)}, u32[]{:S(2)}) copy-start(f32[2,6,256,128]{3,2,1,0:T(8,128)} %get-tuple-element.401) | copy-start | bytes 4718596 | tf_op jit(solution)/shard_map/while/body/eval_jaxpr/cond
  278.0 1.1 copy-start.4
  279.9 8.6 %copy-start.3 = (f32[2,6,256,128]{3,2,1,0:T(8,128)S(1)}, f32[2,6,256,128]{3,2,1,0:T(8,128)}, u32[]{:S(2)}) copy-start(f32[2,6,256,128]{3,2,1,0:T(8,128)} %get-tuple-element.401) | copy-start | bytes 4718596 | tf_op jit(solution)/shard_map/while/body/eval_jaxpr/cond
  300.7 1.1 copy-start.4
  302.7 8.6 %copy-start.3 = (f32[2,6,256,128]{3,2,1,0:T(8,128)S(1)}, f32[2,6,256,128]{3,2,1,0:T(8,128)}, u32[]{:S(2)}) copy-start(f32[2,6,256,128]{3,2,1,0:T(8,128)} %get-tuple-element.401) | copy-start | bytes 4718596 | tf_op jit(solution)/shard_map/while/body/eval_jaxpr/cond
  323.5 1.1 copy-start.4
  325.4 8.6 %copy-start.3 = (f32[2,6,256,128]{3,2,1,0:T(8,128)S(1)}, f32[2,6,256,128]{3,2,1,0:T(8,128)}, u32[]{:S(2)}) copy-start(f32[2,6,256,128]{3,2,1,0:T(8,128)} %get-tuple-element.401) | copy-start | bytes 4718596 | tf_op jit(solution)/shard_map/while/body/eval_jaxpr/cond
  346.2 1.1 copy-start.4
  348.2 8.6 %copy-start.3 = (f32[2,6,256,128]{3,2,1,0:T(8,128)S(1)}, f32[2,6,256,128]{3,2,1,0:T(8,128)}, u32[]{:S(2)}) copy-start(f32[2,6,256,128]{3,2,1,0:T(8,128)} %get-tuple-element.401) | copy-start | bytes 4718596 | tf_op jit(solution)/shard_map/while/body/eval_jaxpr/cond
  369.0 1.1 copy-start.4
  370.9 8.6 %copy-start.3 = (f32[2,6,256,128]{3,2,1,0:T(8,128)S(1)}, f32[2,6,256,128]{3,2,1,0:T(8,128)}, u32[]{:S(2)}) copy-start(f32[2,6,256,128]{3,2,1,0:T(8,128)} %get-tuple-element.401) | copy-start | bytes 4718596 | tf_op jit(solution)/shard_map/while/body/eval_jaxpr/cond
  391.7 1.1 copy-start.4
  393.7 8.6 %copy-start.3 = (f32[2,6,256,128]{3,2,1,0:T(8,128)S(1)}, f32[2,6,256,128]{3,2,1,0:T(8,128)}, u32[]{:S(2)}) copy-start(f32[2,6,256,128]{3,2,1,0:T(8,128)} %get-tuple-element.401) | copy-start | bytes 4718596 | tf_op jit(solution)/shard_map/while/body/eval_jaxpr/cond
  414.5 1.1 copy-start.4
  416.4 8.6 %copy-start.3 = (f32[2,6,256,128]{3,2,1,0:T(8,128)S(1)}, f32[2,6,256,128]{3,2,1,0:T(8,128)}, u32[]{:S(2)}) copy-start(f32[2,6,256,128]{3,2,1,0:T(8,128)} %get-tuple-element.401) | copy-start | bytes 4718596 | tf_op jit(solution)/shard_map/while/body/eval_jaxpr/cond
  437.2 1.1 copy-start.4
  439.2 8.6 %copy-start.3 = (f32[2,6,256,128]{3,2,1,0:T(8,128)S(1)}, f32[2,6,256,128]{3,2,1,0:T(8,128)}, u32[]{:S(2)}) copy-start(f32[2,6,256,128]{3,2,1,0:T(8,128)} %get-tuple-element.401) | copy-start | bytes 4718596 | tf_op jit(solution)/shard_map/while/body/eval_jaxpr/cond
  460.0 1.1 copy-start.4
  461.9 8.6 %copy-start.3 = (f32[2,6,256,128]{3,2,1,0:T(8,128)S(1)}, f32[2,6,256,128]{3,2,1,0:T(8,128)}, u32[]{:S(2)}) copy-start(f32[2,6,256,128]{3,2,1,0:T(8,128)} %get-tuple-element.401) | copy-start | bytes 4718596 | tf_op jit(solution)/shard_map/while/body/eval_jaxpr/cond
  482.7 1.1 copy-start.4
  484.7 8.6 %copy-start.3 = (f32[2,6,256,128]{3,2,1,0:T(8,128)S(1)}, f32[2,6,256,128]{3,2,1,0:T(8,128)}, u32[]{:S(2)}) copy-start(f32[2,6,256,128]{3,2,1,0:T(8,128)} %get-tuple-element.401) | copy-start | bytes 4718596 | tf_op jit(solution)/shard_map/while/body/eval_jaxpr/cond
  505.5 1.1 copy-start.4
  507.4 8.6 %copy-start.3 = (f32[2,6,256,128]{3,2,1,0:T(8,128)S(1)}, f32[2,6,256,128]{3,2,1,0:T(8,128)}, u32[]{:S(2)}) copy-start(f32[2,6,256,128]{3,2,1,0:T(8,128)} %get-tuple-element.401) | copy-start | bytes 4718596 | tf_op jit(solution)/shard_map/while/body/eval_jaxpr/cond
  528.2 1.1 copy-start.4
  530.2 8.6 %copy-start.3 = (f32[2,6,256,128]{3,2,1,0:T(8,128)S(1)}, f32[2,6,256,128]{3,2,1,0:T(8,128)}, u32[]{:S(2)}) copy-start(f32[2,6,256,128]{3,2,1,0:T(8,128)} %get-tuple-element.401) | copy-start | bytes 4718596 | tf_op jit(solution)/shard_map/while/body/eval_jaxpr/cond
  551.0 1.1 copy-start.4
  552.9 8.6 %copy-start.3 = (f32[2,6,256,128]{3,2,1,0:T(8,128)S(1)}, f32[2,6,256,128]{3,2,1,0:T(8,128)}, u32[]{:S(2)}) copy-start(f32[2,6,256,128]{3,2,1,0:T(8,128)} %get-tuple-element.401) | copy-start | bytes 4718596 | tf_op jit(solution)/shard_map/while/body/eval_jaxpr/cond
  573.7 1.1 copy-start.4
  574.9 6.3 %copy-start.5 = (f32[1024]{0:T(1024)S(1)}, f32[1024]{0:T(1024)}, u32[]{:S(2)}) copy-start(f32[1024]{0:T(1024)} %param.18) | copy-start | bytes 12292
  574.9 8.7 %copy-start.1 = (f32[256,1024]{1,0:T(8,128)S(1)}, f32[256,1024]{1,0:T(8,128)}, u32[]{:S(2)}) copy-start(f32[256,1024]{1,0:T(8,128)} %param.14) | copy-start | bytes 3145732
Sparse Core Ops, SparseCore 0:
  14.4 72.5 all-gather.6
  89.2 71.8 all-gather.4
